TPU v7x, 32 devices: a whole 2x2x4 slice. The times are simulated.
32 devices in a mesh: grp: 2 (over y), unit: 4 (over z), period: 2 (over x), rep: 2 (over core).
Axes of the slice: x: 2, y: 2, z: 4, core: 2. Of those that a mesh axis runs over, the one named last changes fastest.
Arguments:
- panel_data: bfloat16 [9216, 2560], P(('grp', 'unit'), ('period', 'rep')), parts along dimension 0, may hold values from -12 to 12
- observed: int32 [9216, 2560], P(('grp', 'unit'), ('period', 'rep')), parts along dimension 0, may hold values 0 or 1
- unit_factors: float32 [9216, 32], P(('grp', 'unit', 'period', 'rep')), parts along dimension 0, may hold values from -6 to 6
- period_factors: float32 [5120, 32], P(('grp', 'period', 'rep')), parts along dimension 0, may hold values from -6 to 6
Outputs:
- unit_result: float32 [9216, 32], P(('grp', 'unit', 'period', 'rep')), parts along dimension 0
- period_result: float32 [5120, 32], P(('grp', 'period', 'rep')), parts along dimension 0
There are 2 independent parts, one for each index of `grp`. A program takes and returns all parts, laid end to end along the dimension named above; each array names one. Nothing has to cross between parts.
All inputs are finite; a program needn't handle non-finite values. No bound on the sum of `observed` on one device may be relied on, other than what follows from the above.
Results may differ from a plain program's by a relative error of at most 0.0039.
Values may be sent and summed in bfloat16 or wider, within the bound.
No kernel may reach another device: no remote copies, remote signals or barrier semaphores. Data moves between devices by JAX's collectives and lax.ppermute only.
A program may use at most 64 MiB of HBM per device.

v0:
```python
import math

import jax
import jax.numpy as jnp
from jax import lax
from jax.sharding import PartitionSpec as P

RANK = 32
ITERS = 2


def masked_residual(panel_data, observed, unit_half, period_half):
    fitted = lax.dot_general(
        unit_half, period_half, (((1,), (1,)), ((), ())), preferred_element_type=jnp.float32
    )
    return (observed.astype(jnp.float32) * (panel_data.astype(jnp.float32) - fitted)).astype(
        jnp.bfloat16
    )


def gather_halves(unit_share):
    return lax.all_gather(unit_share.astype(jnp.bfloat16), ("period", "rep"), axis=0, tiled=True)


def on_device(panel_data, observed, unit_factors, period_factors):
    units = panel_data.shape[0] * lax.axis_size("unit")
    periods = panel_data.shape[1] * lax.axis_size(("period", "rep"))
    unit_rate = 0.5 * math.sqrt(RANK) / periods
    period_rate = 0.5 * math.sqrt(RANK) / units
    unit_share = unit_factors
    period_local = period_factors
    unit_half = gather_halves(unit_share)
    for iteration in range(ITERS):
        period_half = period_local.astype(jnp.bfloat16)
        residual = masked_residual(panel_data, observed, unit_half, period_half)
        picked = residual
        portion = lax.psum_scatter(
            jnp.dot(picked, period_half, preferred_element_type=jnp.float32),
            ("period", "rep"),
            scatter_dimension=0,
            tiled=True,
        )
        unit_share = unit_share + unit_rate * portion
        unit_half = gather_halves(unit_share)
        residual = masked_residual(panel_data, observed, unit_half, period_half)
        partial_sum = lax.dot_general(
            residual, unit_half, (((0,), (0,)), ((), ())), preferred_element_type=jnp.float32
        )
        totals = lax.psum(partial_sum, "unit")
        period_local = period_local + period_rate * totals
    return (unit_share, period_local)


def solution(mesh):
    in_specs = (
        P(("grp", "unit"), ("period", "rep")),
        P(("grp", "unit"), ("period", "rep")),
        P(("grp", "unit", "period", "rep"), None),
        P(("grp", "period", "rep"), None),
    )
    out_specs = (P(("grp", "unit", "period", "rep"), None), P(("grp", "period", "rep"), None))
    return jax.shard_map(
        on_device, mesh=mesh, in_specs=in_specs, out_specs=out_specs, check_vma=False
    )
```

profile of v0, /device:TPU:0, one launch (start us, length us, event | category | flops | bytes accessed | tf_op | source)
XLA Modules:
  0.0 165.2 jit_solution(5813459480691441789)
XLA Ops:
  7.2 0.0 reduce-scatter.7.cloned.1.call-start
  7.2 0.8 convert_bitcast_fusion.2
  8.0 6.3 %all-gather = bf16[4,288,32]{1,2,0:T(8,128)(2,1)S(1)} all-gather(bf16[1,288,32]{1,2,0:T(8,128)(2,1)S(1)} %convert_bitcast_fusion.2), channel_id=1, replica_groups=mesh['grp'=2,'unit'=4,'period'=2,'rep'=2] {'period','rep'}, dimensions={0}, use_global_device_ids=true | all-gather | bytes 92160 | tf_op jit(solution)/shard_map/all_gather | solution.py:22
  14.3 0.1 copy.9
  14.4 0.1 reshape.5
  14.5 0.0 copy-start.2
  14.5 0.0 copy-start
  14.5 0.0 copy-start.1
  14.5 4.3 %fusion.10 = f32[1152,32]{1,0:T(8,128)} fusion(bf16[1152,32]{0,1:T(8,128)(2,1)S(1)} %reshape.5, bf16[1152,640]{1,0:T(8,128)(2,1)} %param.4, s32[1152,640]{1,0:T(8,128)} %param.5, f32[640,32]{0,1:T(8,128)} %param.7), kind=kOutput, calls=%fused_computation.14 | convolution fusion | flops 98099200 | bytes 4726784
  18.8 0.0 reduce-scatter.7.cloned.1.call-update
  18.8 0.0 all-reduce.3.cloned.1.call-start
  18.9 23.9 %reduce-scatter.7.cloned.1.call-done = f32[288,32]{1,0:T(8,128)} async-done(((f32[1152,32]{1,0:T(8,128)}), f32[288,32]{1,0:T(8,128)}) %reduce-scatter.7.cloned.1.call-update) | async-done | bytes 36880
  42.8 1.0 copy.13
  43.8 0.0 copy-done.2
  43.8 5.3 %all-gather.1 = bf16[4,288,32]{1,2,0:T(8,128)(2,1)S(1)} all-gather(bf16[1,288,32]{1,2,0:T(8,128)(2,1)S(1)} %convert_bitcast_fusion.1), channel_id=1, replica_groups=mesh['grp'=2,'unit'=4,'period'=2,'rep'=2] {'period','rep'}, dimensions={0}, use_global_device_ids=true | all-gather | bytes 92160 | tf_op jit(solution)/shard_map/all_gather | solution.py:22
  49.2 0.1 copy.10
  49.2 0.1 reshape.7
  49.3 0.0 copy-done
  49.4 0.0 copy-done.1
  49.4 2.9 %fusion.8 = f32[640,32]{0,1:T(8,128)} fusion(bf16[1152,32]{0,1:T(8,128)(2,1)S(1)} %reshape.7, bf16[1152,640]{1,0:T(8,128)(2,1)} %param.4, s32[1152,640]{1,0:T(8,128)S(1)} %copy-done, f32[640,32]{0,1:T(8,128)S(1)} %copy-done.1), kind=kOutput, calls=%fused_computation.12 | convolution fusion | flops 98078720 | bytes 4661248 | tf_op jit(solution)/shard_map/dot_general | solution.py:46
  52.3 0.0 all-reduce.3.cloned.1.call-update
  52.3 0.0 reduce-scatter.9.cloned.1.call-start
  52.3 34.1 %all-reduce.3.cloned.1.call-done = f32[640,32]{0,1:T(8,128)} async-done(((f32[640,32]{0,1:T(8,128)}), f32[640,32]{0,1:T(8,128)}) %all-reduce.3.cloned.1.call-update) | async-done | bytes 81936 | tf_op jit(solution)/shard_map/psum | solution.py:49
  86.4 0.9 fusion.12
  87.3 3.2 %fusion.11 = f32[1152,32]{1,0:T(8,128)} fusion(bf16[640,32]{0,1:T(8,128)(2,1)S(1)} %fusion.12, bf16[1152,32]{0,1:T(8,128)(2,1)S(1)} %reshape.7, bf16[1152,640]{1,0:T(8,128)(2,1)} %param.4, s32[1152,640]{1,0:T(8,128)S(1)} %copy-done), kind=kOutput, calls=%fused_computation.15 | convolution fusion | flops 98058240 | bytes 4685824
  90.6 0.0 reduce-scatter.9.cloned.1.call-update
  90.6 0.0 copy-start.3
  90.6 0.0 all-reduce.5.cloned.1.call-start
  90.7 22.2 %reduce-scatter.9.cloned.1.call-done = f32[288,32]{1,0:T(8,128)} async-done(((f32[1152,32]{1,0:T(8,128)}), f32[288,32]{1,0:T(8,128)}) %reduce-scatter.9.cloned.1.call-update) | async-done | bytes 36880
  112.8 1.0 copy.15
  113.8 0.7 convert_bitcast_fusion
  114.5 5.3 %all-gather.2 = bf16[4,288,32]{1,2,0:T(8,128)(2,1)S(1)} all-gather(bf16[1,288,32]{1,2,0:T(8,128)(2,1)S(1)} %get-tuple-element.2), channel_id=1, replica_groups=mesh['grp'=2,'unit'=4,'period'=2,'rep'=2] {'period','rep'}, dimensions={0}, use_global_device_ids=true | all-gather | bytes 92160 | tf_op jit(solution)/shard_map/all_gather | solution.py:22
  119.8 0.1 copy.11
  119.9 0.1 reshape.9
  120.0 2.9 %fusion.9 = f32[640,32]{0,1:T(8,128)} fusion(bf16[1152,32]{0,1:T(8,128)(2,1)S(1)} %reshape.9, bf16[640,32]{0,1:T(8,128)(2,1)S(1)} %fusion.12, bf16[1152,640]{1,0:T(8,128)(2,1)} %param.4, s32[1152,640]{1,0:T(8,128)S(1)} %copy-done), kind=kOutput, calls=%fused_computation.13 | convolution fusion | flops 98058240 | bytes 4620288 | tf_op jit(solution)/shard_map/dot_general | solution.py:46
  122.9 0.0 all-reduce.5.cloned.1.call-update
  122.9 34.2 %all-reduce.5.cloned.1.call-done = f32[640,32]{0,1:T(8,128)} async-done(((f32[640,32]{0,1:T(8,128)}), f32[640,32]{0,1:T(8,128)}) %all-reduce.5.cloned.1.call-update) | async-done | bytes 81936 | tf_op jit(solution)/shard_map/psum | solution.py:49
  157.1 0.0 copy-done.3
  157.1 1.5 multiply_add_fusion
  (1 shorter events, 0.0 us)
Async XLA Ops:
  7.2 35.6 %reduce-scatter.7.cloned.1.call-start = ((), (), s32[]{:S(2)}) async-start(), calls=%async_computation.4 | async-start | bytes 737280
  14.5 29.3 %copy-start.2 = (f32[288,32]{0,1:T(8,128)S(1)}, f32[288,32]{0,1:T(8,128)}, u32[]{:S(2)}) copy-start(f32[288,32]{0,1:T(8,128)} %param.6) | copy-start | bytes 110596
  14.5 34.9 %copy-start = (s32[1152,640]{1,0:T(8,128)S(1)}, s32[1152,640]{1,0:T(8,128)}, u32[]{:S(2)}) copy-start(s32[1152,640]{1,0:T(8,128)} %param.5) | copy-start | bytes 8847364
  14.5 34.9 %copy-start.1 = (f32[640,32]{0,1:T(8,128)S(1)}, f32[640,32]{0,1:T(8,128)}, u32[]{:S(2)}) copy-start(f32[640,32]{0,1:T(8,128)} %param.7) | copy-start | bytes 245764
  18.8 67.6 %all-reduce.3.cloned.1.call-start = ((), (), s32[]{:S(2)}) async-start(), calls=%async_computation.2 | async-start | bytes 163840 | tf_op jit(solution)/shard_map/psum | solution.py:49
  52.3 60.5 %reduce-scatter.9.cloned.1.call-start = ((), (), s32[]{:S(2)}) async-start(), calls=%async_computation.5 | async-start | bytes 737280
  90.6 66.5 %copy-start.3 = (f32[640,32]{0,1:T(8,128)S(1)}, f32[640,32]{0,1:T(8,128)}, u32[]{:S(2)}) copy-start(f32[640,32]{0,1:T(8,128)} %all-reduce.3.cloned.1.call-done) | copy-start | bytes 245764
  90.6 66.5 %all-reduce.5.cloned.1.call-start = ((), (), s32[]{:S(2)}) async-start(), calls=%async_computation.3 | async-start | bytes 163840 | tf_op jit(solution)/shard_map/psum | solution.py:49
Sparse Core Ops, SparseCore 0:
  19.0 23.8 reduce-scatter.6
  52.4 33.9 all-reduce.2
  90.7 22.0 reduce-scatter.8
  123.1 34.0 all-reduce.4
where the time goes:
time: 166 us; the launch traced here: 165 us
  waiting for transfers between devices  114 us (69%)
  blocking collectives  16.9 us (10%)
  between operations  13.8 us (8%)
  matrix products  13.3 us (8%)
  other arithmetic  3.92 us (2%)
  local copies, waits for them, and re-layouts  2.55 us (2%)
    psum x2, waiting for transfers between devices, on_device(): totals = lax.psum(partial_sum, 'unit')  68.3 us
    unnamed x6, waiting for transfers between devices  46.2 us
    all_gather x3, blocking collectives, gather_halves(): lax.all_gather(unit_share.astype(jnp.bfloat16), ('period', 'rep'), axis=0...  16.9 us
    unnamed x2, matrix products  7.51 us
    dot_general x2, matrix products, on_device(): lax.dot_general(residual, unit_half, (((0,), (0,)), ((), ())), preferred_...  5.83 us
  transfers between devices with their start and end apart: 4, of which 4 were waited for; matrix products, arithmetic and copies ran while one was open for 0% of the time, Pallas kernels for 0%

commit v1 on v0

v1 whole, which is shorter than its diff:
```python
import functools
import math

import jax
import jax.numpy as jnp
from jax import lax
from jax.experimental import pallas as pl
from jax.experimental.pallas import tpu as pltpu
from jax.sharding import PartitionSpec as P

RANK = 32
ITERS = 2
F32, BF16 = jnp.float32, jnp.bfloat16
SHARE = ("period", "rep")
WHOLE = pl.BlockSpec(memory_space=pltpu.VMEM)


def swap_all(block, axes):
    size = lax.axis_size(axes)
    return [
        lax.ppermute(block, axes, [(i, i ^ step) for i in range(size)]) for step in range(1, size)
    ]


def tree_sum(refs):
    blocks = [ref[...].astype(F32) for ref in refs]
    while len(blocks) > 1:
        blocks = [a + b for a, b in zip(blocks[::2], blocks[1::2])]
    return blocks[0]


def masked_residual(units, periods, panel, mask):
    fitted = lax.dot_general(units, periods, (((0,), (0,)), ((), ())), preferred_element_type=F32)
    return (panel.astype(F32) - fitted).astype(BF16) * mask


def unit_partial(units, periods, panel, mask):
    residual = masked_residual(units, periods, panel, mask)
    return lax.dot_general(
        periods, residual, (((1,), (1,)), ((), ())), preferred_element_type=F32
    ).astype(BF16)


def first_unit_kernel(*refs):
    *shares, period, panel, observed, mask, unit, part, rows = refs
    me = lax.axis_index(SHARE)
    size = shares[0].shape[1]
    for step, share in enumerate(shares):
        rows[pl.ds((me ^ step) * size, size), :] = share[...].T
    whole = rows[...].T
    unit[...] = whole
    mask[...] = observed[...].astype(F32).astype(BF16)
    part[...] = unit_partial(
        whole.astype(BF16), period[...].astype(BF16), panel[...], mask[...]
    )


def period_kernel(rate, *refs):
    *parts, unit, period, panel, mask, new_unit, part = refs
    whole = unit[...] + rate * tree_sum(parts)
    new_unit[...] = whole
    units = whole.astype(BF16)
    residual = masked_residual(units, period[...].astype(BF16), panel[...], mask[...])
    part[...] = jnp.dot(units, residual, preferred_element_type=F32).astype(BF16)


def unit_kernel(rate, *refs):
    *parts, unit, period, panel, mask, new_period, part = refs
    whole = period[...] + rate * tree_sum(parts)
    new_period[...] = whole
    part[...] = unit_partial(
        unit[...].astype(BF16), whole.astype(BF16), panel[...], mask[...]
    )


def share_kernel(unit, share, rows):
    size = share.shape[1]
    rows[...] = unit[...].T
    share[...] = rows[pl.ds(lax.axis_index(SHARE) * size, size), :].T


def last_period_kernel(rate, *refs):
    *parts, period, new_period = refs
    new_period[...] = period[...] + rate * tree_sum(parts)


def call(kernel, outs, args, scratch=()):
    return pl.pallas_call(
        kernel,
        in_specs=[WHOLE] * len(args),
        out_specs=[WHOLE] * len(outs),
        out_shape=[jax.ShapeDtypeStruct(shape, dtype) for shape, dtype in outs],
        scratch_shapes=[pltpu.VMEM(shape, dtype) for shape, dtype in scratch],
        compiler_params=pltpu.CompilerParams(vmem_limit_bytes=24 * 2**20),
    )(*args)


def on_device(panel, observed, unit_factors, period_factors):
    units, periods = panel.shape
    unit_rate = 0.5 * math.sqrt(RANK) / (periods * lax.axis_size(SHARE))
    period_rate = 0.5 * math.sqrt(RANK) / (units * lax.axis_size("unit"))
    unit_like, period_like = (RANK, units), (RANK, periods)

    own = unit_factors.T
    period = period_factors.T
    mask, unit, part = call(
        first_unit_kernel,
        [(panel.shape, BF16), (unit_like, F32), (unit_like, BF16)],
        [own, *swap_all(own, SHARE), period, panel, observed],
        [((units, RANK), F32)],
    )
    for iteration in range(ITERS):
        unit, sums = call(
            functools.partial(period_kernel, unit_rate),
            [(unit_like, F32), (period_like, BF16)],
            [part, *swap_all(part, SHARE), unit, period, panel, mask],
        )
        if iteration < ITERS - 1:
            period, part = call(
                functools.partial(unit_kernel, period_rate),
                [(period_like, F32), (unit_like, BF16)],
                [sums, *swap_all(sums, "unit"), unit, period, panel, mask],
            )
    (share,) = call(share_kernel, [(own.shape, F32)], [unit], [((units, RANK), F32)])
    (period,) = call(
        functools.partial(last_period_kernel, period_rate),
        [(period_like, F32)],
        [sums, *swap_all(sums, "unit"), period],
    )
    return share.T, period.T


def solution(mesh):
    in_specs = (
        P(("grp", "unit"), ("period", "rep")),
        P(("grp", "unit"), ("period", "rep")),
        P(("grp", "unit", "period", "rep"), None),
        P(("grp", "period", "rep"), None),
    )
    out_specs = (P(("grp", "unit", "period", "rep"), None), P(("grp", "period", "rep"), None))
    return jax.shard_map(
        on_device, mesh=mesh, in_specs=in_specs, out_specs=out_specs, check_vma=False
    )
```

time: 166 us -> 45.7 us (0.28)
  waiting for transfers between devices: 114 us -> 18.1 us
  blocking collectives: 16.9 us -> 0 us
  starting transfers between devices: 0.16 us -> 15.9 us
  matrix products: 13.3 us -> 0 us
  between operations: 13.8 us -> 0.69 us
  Pallas kernels: 0 us -> 5.83 us
  other arithmetic: 3.92 us -> 0 us
  local copies, waits for them, and re-layouts: 2.55 us -> 4.89 us
    psum x2 -> x0, waiting for transfers between devices: 68.3 us -> none  [on_device(): totals = lax.psum(partial_sum, 'unit')]
    unnamed x6 -> x0, waiting for transfers between devices: 46.2 us -> none
    ppermute x0 -> x15, waiting for transfers between devices: none -> 18.1 us  [swap_all(): lax.ppermute(block, axes, [(i, i ^ step) for i in range(size)])]
    all_gather x3 -> x0, blocking collectives: 16.9 us -> none  [gather_halves(): lax.all_gather(unit_share.astype(jnp.bfloat16), ('period', 'rep'), axis=0...]
    ppermute x0 -> x15, starting transfers between devices: none -> 15.9 us  [swap_all(): lax.ppermute(block, axes, [(i, i ^ step) for i in range(size)])]
    unnamed x2 -> x0, matrix products: 7.51 us -> none
    dot_general x2 -> x0, matrix products: 5.83 us -> none  [on_device(): lax.dot_general(residual, unit_half, (((0,), (0,)), ((), ())), preferred_...]
    pallas_call x0 -> x6, Pallas kernels: none -> 5.83 us  [call(): pl.pallas_call(kernel, in_specs=[WHOLE] * len(args), out_specs=[WHOLE] *...]
  transfers between devices with their start and end apart: 4 -> 15, of which waited for: 4 -> 10; matrix products, arithmetic and copies ran while one was open for 0% -> 0% of each run, Pallas kernels for 0% -> 2%
where the time goes in v1:
time: 45.7 us; the launch traced here: 45.4 us
  waiting for transfers between devices  18.1 us (40%)
  starting transfers between devices  15.9 us (35%)
  Pallas kernels  5.83 us (13%)
  local copies, waits for them, and re-layouts  4.89 us (11%)
  between operations  0.69 us (2%)
    ppermute x15, waiting for transfers between devices, swap_all(): lax.ppermute(block, axes, [(i, i ^ step) for i in range(size)])  18.1 us
    ppermute x15, starting transfers between devices, swap_all(): lax.ppermute(block, axes, [(i, i ^ step) for i in range(size)])  15.9 us
    pallas_call x6, Pallas kernels, call(): pl.pallas_call(kernel, in_specs=[WHOLE] * len(args), out_specs=[WHOLE] *...  5.83 us
    unnamed x10, local copies, waits for them, and re-layouts  4.89 us
  transfers between devices with their start and end apart: 15, of which 10 were waited for; matrix products, arithmetic and copies ran while one was open for 0% of the time, Pallas kernels for 2%

profile of v1, /device:TPU:0, one launch (start us, length us, event | category | flops | bytes accessed | tf_op | source)
XLA Modules:
  0.0 45.4 jit_solution(16427948922370753825)
XLA Ops:
  0.6 2.4 %collective-permute-start.2 = (f32[32,288]{1,0:T(8,128)}, f32[32,288]{1,0:T(8,128)S(1)}, u32[]{:S(2)}, u32[]{:S(2)}) collective-permute-start(f32[32,288]{1,0:T(8,128)} %bitcast.7), channel_id=1, source_target_pairs={{0,3},{1,2},{2,1},{3,0},{4,7},{5,6},{6,5},{7,4},{8,11},{9,10},{10,... | collective-permute-start | bytes 110600 | tf_op jit(solution)/shard_map/ppermute | solution.py:21
  3.1 0.6 %collective-permute-start.1 = (f32[32,288]{1,0:T(8,128)}, f32[32,288]{1,0:T(8,128)S(1)}, u32[]{:S(2)}, u32[]{:S(2)}) collective-permute-start(f32[32,288]{1,0:T(8,128)} %bitcast.8), channel_id=1, source_target_pairs={{0,2},{1,3},{2,0},{3,1},{4,6},{5,7},{6,4},{7,5},{8,10},{9,11},{10,... | collective-permute-start | bytes 110600 | tf_op jit(solution)/shard_map/ppermute | solution.py:21
  3.7 0.0 collective-permute-start
  3.8 1.8 %collective-permute-done.2.refs_3_ = f32[32,288]{1,0:T(8,128)S(1)} collective-permute-done((f32[32,288]{1,0:T(8,128)}, f32[32,288]{1,0:T(8,128)S(1)}, u32[]{:S(2)}, u32[]{:S(2)}) %collective-permute-start.2) | collective-permute-done | bytes 36896 | tf_op jit(solution)/shard_map/ppermute | solution.py:21
  5.5 2.1 %collective-permute-done.1.refs_2_ = f32[32,288]{1,0:T(8,128)S(1)} collective-permute-done((f32[32,288]{1,0:T(8,128)}, f32[32,288]{1,0:T(8,128)S(1)}, u32[]{:S(2)}, u32[]{:S(2)}) %collective-permute-start.1) | collective-permute-done | bytes 36896 | tf_op jit(solution)/shard_map/ppermute | solution.py:21
  7.6 0.0 collective-permute-done.refs_1_
  7.6 0.0 copy-start
  7.6 1.4 %copy-done = bf16[1152,640]{1,0:T(8,128)(2,1)S(1)} copy-done((bf16[1152,640]{1,0:T(8,128)(2,1)S(1)}, bf16[1152,640]{1,0:T(8,128)(2,1)}, u32[]{:S(2)}) %copy-start) | copy-done | bytes 1474584
  9.0 0.0 copy-start.2
  9.0 1.8 %copy-done.2 = s32[1152,640]{1,0:T(8,128)S(1)} copy-done((s32[1152,640]{1,0:T(8,128)S(1)}, s32[1152,640]{1,0:T(8,128)}, u32[]{:S(2)}) %copy-start.2) | copy-done | bytes 2949144
  10.8 0.0 copy-start.3
  10.8 0.9 %copy-done.3 = f32[640,32]{0,1:T(8,128)S(1)} copy-done((f32[640,32]{0,1:T(8,128)S(1)}, f32[640,32]{0,1:T(8,128)}, u32[]{:S(2)}) %copy-start.3) | copy-done | bytes 81944
  11.7 0.0 copy-start.4
  11.7 0.8 %copy-done.4 = f32[288,32]{0,1:T(8,128)S(1)} copy-done((f32[288,32]{0,1:T(8,128)S(1)}, f32[288,32]{0,1:T(8,128)}, u32[]{:S(2)}) %copy-start.4) | copy-done | bytes 36888
  12.5 0.0 copy-start.1
  12.5 1.6 %shard_map.59 = (bf16[1152,640]{1,0:T(8,128)(2,1)S(1)}, f32[32,1152]{1,0:T(8,128)S(1)}, bf16[32,1152]{1,0:T(8,128)(2,1)S(1)}) custom-call(f32[32,288]{1,0:T(8,128)S(1)} %bitcast.10, f32[32,288]{1,0:T(8,128)S(1)} %collective-permute-done.refs_1_, f32[32,288]{1,0:T(8,128)S(1)} %collective-permute-done.1.refs_2_, f32[32,288]{1,0:T(8,128)S(1)} %collective-permute-done.2.refs_3_, ...), custom_call_target="tpu_custom_call" | custom-call | tf_op jit(solution)/shard_map/pallas_call | solution.py:88
  14.1 1.1 %collective-permute-start.5 = (bf16[32,1152]{1,0:T(8,128)(2,1)S(1)}, bf16[32,1152]{1,0:T(8,128)(2,1)S(1)}, u32[]{:S(2)}, u32[]{:S(2)}) collective-permute-start(bf16[32,1152]{1,0:T(8,128)(2,1)S(1)} %get-tuple-element.11.refs_0_), channel_id=1, source_target_pairs={{0,3},{1,2},{2,1},{3,0},{4,7},{5,6},{6,5},{7,4},{8,11},{9,10},{10,... | collective-permute-start | bytes 221192 | tf_op jit(solution)/shard_map/ppermute | solution.py:21
  15.2 0.4 collective-permute-start.4
  15.7 0.4 collective-permute-start.3
  16.1 2.7 %collective-permute-done.5.refs_3_ = bf16[32,1152]{1,0:T(8,128)(2,1)S(1)} collective-permute-done((bf16[32,1152]{1,0:T(8,128)(2,1)S(1)}, bf16[32,1152]{1,0:T(8,128)(2,1)S(1)}, u32[]{:S(2)}, u32[]{:S(2)}) %collective-permute-start.5) | collective-permute-done | bytes 73760 | tf_op jit(solution)/shard_map/ppermute | solution.py:21
  18.8 1.6 %collective-permute-done.4.refs_2_ = bf16[32,1152]{1,0:T(8,128)(2,1)S(1)} collective-permute-done((bf16[32,1152]{1,0:T(8,128)(2,1)S(1)}, bf16[32,1152]{1,0:T(8,128)(2,1)S(1)}, u32[]{:S(2)}, u32[]{:S(2)}) %collective-permute-start.4) | collective-permute-done | bytes 73760 | tf_op jit(solution)/shard_map/ppermute | solution.py:21
  20.4 0.0 collective-permute-done.3.refs_1_
  20.4 0.0 copy-done.1
  20.4 0.8 %shard_map.60 = (f32[32,1152]{1,0:T(8,128)S(1)}, bf16[32,640]{1,0:T(8,128)(2,1)S(1)}) custom-call(bf16[32,1152]{1,0:T(8,128)(2,1)S(1)} %get-tuple-element.11.refs_0_, bf16[32,1152]{1,0:T(8,128)(2,1)S(1)} %collective-permute-done.3.refs_1_, bf16[32,1152]{1,0:T(8,128)(2,1)S(1)} %collective-permute-done.4.refs_2_, ...), custom_call_target="tpu_custom_call" | custom-call | tf_op jit(solution)/shard_map/pallas_call | solution.py:88
  21.2 3.7 %collective-permute-start.8 = (bf16[32,640]{1,0:T(8,128)(2,1)S(1)}, bf16[32,640]{1,0:T(8,128)(2,1)S(1)}, u32[]{:S(2)}, u32[]{:S(2)}) collective-permute-start(bf16[32,640]{1,0:T(8,128)(2,1)S(1)} %get-tuple-element.14.refs_0_), channel_id=1, source_target_pairs={{0,12},{4,8},{8,4},{12,0},{1,13},{5,9},{9,5},{13,1},{2,14},{6,10},... | collective-permute-start | bytes 122888 | tf_op jit(solution)/shard_map/ppermute | solution.py:21
  24.9 0.0 collective-permute-start.7
  24.9 0.8 %collective-permute-start.6 = (bf16[32,640]{1,0:T(8,128)(2,1)S(1)}, bf16[32,640]{1,0:T(8,128)(2,1)S(1)}, u32[]{:S(2)}, u32[]{:S(2)}) collective-permute-start(bf16[32,640]{1,0:T(8,128)(2,1)S(1)} %get-tuple-element.14.refs_0_), channel_id=1, source_target_pairs={{0,4},{4,0},{8,12},{12,8},{1,5},{5,1},{9,13},{13,9},{2,6},{6,2},{1... | collective-permute-start | bytes 122888 | tf_op jit(solution)/shard_map/ppermute | solution.py:21
  25.6 1.4 %collective-permute-done.8.refs_3_ = bf16[32,640]{1,0:T(8,128)(2,1)S(1)} collective-permute-done((bf16[32,640]{1,0:T(8,128)(2,1)S(1)}, bf16[32,640]{1,0:T(8,128)(2,1)S(1)}, u32[]{:S(2)}, u32[]{:S(2)}) %collective-permute-start.8) | collective-permute-done | bytes 40992 | tf_op jit(solution)/shard_map/ppermute | solution.py:21
  27.1 2.7 %collective-permute-done.7.refs_2_ = bf16[32,640]{1,0:T(8,128)(2,1)S(1)} collective-permute-done((bf16[32,640]{1,0:T(8,128)(2,1)S(1)}, bf16[32,640]{1,0:T(8,128)(2,1)S(1)}, u32[]{:S(2)}, u32[]{:S(2)}) %collective-permute-start.7) | collective-permute-done | bytes 40992 | tf_op jit(solution)/shard_map/ppermute | solution.py:21
  29.8 0.0 collective-permute-done.6.refs_1_
  29.8 0.9 %shard_map.61 = (f32[32,640]{1,0:T(8,128)S(1)}, bf16[32,1152]{1,0:T(8,128)(2,1)S(1)}) custom-call(bf16[32,640]{1,0:T(8,128)(2,1)S(1)} %get-tuple-element.14.refs_0_, bf16[32,640]{1,0:T(8,128)(2,1)S(1)} %collective-permute-done.6.refs_1_, bf16[32,640]{1,0:T(8,128)(2,1)S(1)} %collective-permute-done.7.refs_2_, ...), custom_call_target="tpu_custom_call" | custom-call | tf_op jit(solution)/shard_map/pallas_call | solution.py:88
  30.7 0.1 collective-permute-start.11
  30.8 1.4 %collective-permute-start.10 = (bf16[32,1152]{1,0:T(8,128)(2,1)S(1)}, bf16[32,1152]{1,0:T(8,128)(2,1)S(1)}, u32[]{:S(2)}, u32[]{:S(2)}) collective-permute-start(bf16[32,1152]{1,0:T(8,128)(2,1)S(1)} %get-tuple-element.16.refs_0_), channel_id=1, source_target_pairs={{0,2},{1,3},{2,0},{3,1},{4,6},{5,7},{6,4},{7,5},{8,10},{9,11},{10,... | collective-permute-start | bytes 221192 | tf_op jit(solution)/shard_map/ppermute | solution.py:21
  32.2 0.5 %collective-permute-start.9 = (bf16[32,1152]{1,0:T(8,128)(2,1)S(1)}, bf16[32,1152]{1,0:T(8,128)(2,1)S(1)}, u32[]{:S(2)}, u32[]{:S(2)}) collective-permute-start(bf16[32,1152]{1,0:T(8,128)(2,1)S(1)} %get-tuple-element.16.refs_0_), channel_id=1, source_target_pairs={{0,1},{1,0},{2,3},{3,2},{4,5},{5,4},{6,7},{7,6},{8,9},{9,8},{10,11... | collective-permute-start | bytes 221192 | tf_op jit(solution)/shard_map/ppermute | solution.py:21
  32.6 2.7 %collective-permute-done.11.refs_3_ = bf16[32,1152]{1,0:T(8,128)(2,1)S(1)} collective-permute-done((bf16[32,1152]{1,0:T(8,128)(2,1)S(1)}, bf16[32,1152]{1,0:T(8,128)(2,1)S(1)}, u32[]{:S(2)}, u32[]{:S(2)}) %collective-permute-start.11) | collective-permute-done | bytes 73760 | tf_op jit(solution)/shard_map/ppermute | solution.py:21
  35.3 1.3 %collective-permute-done.10.refs_2_ = bf16[32,1152]{1,0:T(8,128)(2,1)S(1)} collective-permute-done((bf16[32,1152]{1,0:T(8,128)(2,1)S(1)}, bf16[32,1152]{1,0:T(8,128)(2,1)S(1)}, u32[]{:S(2)}, u32[]{:S(2)}) %collective-permute-start.10) | collective-permute-done | bytes 73760 | tf_op jit(solution)/shard_map/ppermute | solution.py:21
  36.7 0.0 collective-permute-done.9.refs_1_
  36.7 0.8 %shard_map.62 = (f32[32,1152]{1,0:T(8,128)S(1)}, bf16[32,640]{1,0:T(8,128)(2,1)S(1)}) custom-call(bf16[32,1152]{1,0:T(8,128)(2,1)S(1)} %get-tuple-element.16.refs_0_, bf16[32,1152]{1,0:T(8,128)(2,1)S(1)} %collective-permute-done.9.refs_1_, bf16[32,1152]{1,0:T(8,128)(2,1)S(1)} %collective-permute-done.10.refs_2_, ...), custom_call_target="tpu_custom_call" | custom-call | tf_op jit(solution)/shard_map/pallas_call | solution.py:88
  37.5 1.5 %collective-permute-start.14 = (bf16[32,640]{1,0:T(8,128)(2,1)S(1)}, bf16[32,640]{1,0:T(8,128)(2,1)S(1)}, u32[]{:S(2)}, u32[]{:S(2)}) collective-permute-start(bf16[32,640]{1,0:T(8,128)(2,1)S(1)} %get-tuple-element.19.refs_0_), channel_id=1, source_target_pairs={{0,12},{4,8},{8,4},{12,0},{1,13},{5,9},{9,5},{13,1},{2,14},{6,10},... | collective-permute-start | bytes 122888 | tf_op jit(solution)/shard_map/ppermute | solution.py:21
  39.0 0.7 %collective-permute-start.13 = (bf16[32,640]{1,0:T(8,128)(2,1)S(1)}, bf16[32,640]{1,0:T(8,128)(2,1)S(1)}, u32[]{:S(2)}, u32[]{:S(2)}) collective-permute-start(bf16[32,640]{1,0:T(8,128)(2,1)S(1)} %get-tuple-element.19.refs_0_), channel_id=1, source_target_pairs={{0,8},{4,12},{8,0},{12,4},{1,9},{5,13},{9,1},{13,5},{2,10},{6,14},... | collective-permute-start | bytes 122888 | tf_op jit(solution)/shard_map/ppermute | solution.py:21
  39.7 2.3 %collective-permute-start.12 = (bf16[32,640]{1,0:T(8,128)(2,1)S(1)}, bf16[32,640]{1,0:T(8,128)(2,1)S(1)}, u32[]{:S(2)}, u32[]{:S(2)}) collective-permute-start(bf16[32,640]{1,0:T(8,128)(2,1)S(1)} %get-tuple-element.19.refs_0_), channel_id=1, source_target_pairs={{0,4},{4,0},{8,12},{12,8},{1,5},{5,1},{9,13},{13,9},{2,6},{6,2},{1... | collective-permute-start | bytes 122888 | tf_op jit(solution)/shard_map/ppermute | solution.py:21
  42.0 1.0 %shard_map.63 = f32[32,288]{1,0:T(8,128)} custom-call(f32[32,1152]{1,0:T(8,128)S(1)} %get-tuple-element.18.unit), custom_call_target="tpu_custom_call" | custom-call | tf_op jit(solution)/shard_map/pallas_call | solution.py:88
  42.9 0.9 %collective-permute-done.14.refs_3_ = bf16[32,640]{1,0:T(8,128)(2,1)S(1)} collective-permute-done((bf16[32,640]{1,0:T(8,128)(2,1)S(1)}, bf16[32,640]{1,0:T(8,128)(2,1)S(1)}, u32[]{:S(2)}, u32[]{:S(2)}) %collective-permute-start.14) | collective-permute-done | bytes 40992 | tf_op jit(solution)/shard_map/ppermute | solution.py:21
  43.8 0.9 %collective-permute-done.13.refs_2_ = bf16[32,640]{1,0:T(8,128)(2,1)S(1)} collective-permute-done((bf16[32,640]{1,0:T(8,128)(2,1)S(1)}, bf16[32,640]{1,0:T(8,128)(2,1)S(1)}, u32[]{:S(2)}, u32[]{:S(2)}) %collective-permute-start.13) | collective-permute-done | bytes 40992 | tf_op jit(solution)/shard_map/ppermute | solution.py:21
  44.7 0.0 collective-permute-done.12.refs_1_
  44.7 0.7 %shard_map.64 = f32[32,640]{1,0:T(8,128)} custom-call(bf16[32,640]{1,0:T(8,128)(2,1)S(1)} %get-tuple-element.19.refs_0_, bf16[32,640]{1,0:T(8,128)(2,1)S(1)} %collective-permute-done.12.refs_1_, bf16[32,640]{1,0:T(8,128)(2,1)S(1)} %collective-permute-done.13.refs_2_, bf16[32,640]{1,0:T(8,128)(2,1)S(1)} %collective-permute-done.14.refs_3_, ...), custom_call_target="tpu_custom_call" | custom-call | tf_op jit(solution)/shard_map/pallas_call | solution.py:88
Async XLA Ops:
  0.6 4.9 %collective-permute-start.2 = (f32[32,288]{1,0:T(8,128)}, f32[32,288]{1,0:T(8,128)S(1)}, u32[]{:S(2)}, u32[]{:S(2)}) collective-permute-start(f32[32,288]{1,0:T(8,128)} %bitcast.7), channel_id=1, source_target_pairs={{0,3},{1,2},{2,1},{3,0},{4,7},{5,6},{6,5},{7,4},{8,11},{9,10},{10,... | collective-permute-start | bytes 110600 | tf_op jit(solution)/shard_map/ppermute | solution.py:21
  3.1 4.5 %collective-permute-start.1 = (f32[32,288]{1,0:T(8,128)}, f32[32,288]{1,0:T(8,128)S(1)}, u32[]{:S(2)}, u32[]{:S(2)}) collective-permute-start(f32[32,288]{1,0:T(8,128)} %bitcast.8), channel_id=1, source_target_pairs={{0,2},{1,3},{2,0},{3,1},{4,6},{5,7},{6,4},{7,5},{8,10},{9,11},{10,... | collective-permute-start | bytes 110600 | tf_op jit(solution)/shard_map/ppermute | solution.py:21
  3.7 3.9 %collective-permute-start = (f32[32,288]{1,0:T(8,128)}, f32[32,288]{1,0:T(8,128)S(1)}, u32[]{:S(2)}, u32[]{:S(2)}) collective-permute-start(f32[32,288]{1,0:T(8,128)} %bitcast.9), channel_id=1, source_target_pairs={{0,1},{1,0},{2,3},{3,2},{4,5},{5,4},{6,7},{7,6},{8,9},{9,8},{10,11... | collective-permute-start | bytes 110600 | tf_op jit(solution)/shard_map/ppermute | solution.py:21
  7.6 1.4 %copy-start = (bf16[1152,640]{1,0:T(8,128)(2,1)S(1)}, bf16[1152,640]{1,0:T(8,128)(2,1)}, u32[]{:S(2)}) copy-start(bf16[1152,640]{1,0:T(8,128)(2,1)} %refs_6_.7) | copy-start | bytes 4423684
  9.0 1.8 %copy-start.2 = (s32[1152,640]{1,0:T(8,128)S(1)}, s32[1152,640]{1,0:T(8,128)}, u32[]{:S(2)}) copy-start(s32[1152,640]{1,0:T(8,128)} %refs_6_.4) | copy-start | bytes 8847364
  10.8 0.9 %copy-start.3 = (f32[640,32]{0,1:T(8,128)S(1)}, f32[640,32]{0,1:T(8,128)}, u32[]{:S(2)}) copy-start(f32[640,32]{0,1:T(8,128)} %param.7) | copy-start | bytes 245764
  11.7 0.8 %copy-start.4 = (f32[288,32]{0,1:T(8,128)S(1)}, f32[288,32]{0,1:T(8,128)}, u32[]{:S(2)}) copy-start(f32[288,32]{0,1:T(8,128)} %param.6) | copy-start | bytes 110596
  12.5 7.9 %copy-start.1 = (bf16[1152,640]{1,0:T(8,128)(2,1)S(1)}, bf16[1152,640]{1,0:T(8,128)(2,1)}, u32[]{:S(2)}) copy-start(bf16[1152,640]{1,0:T(8,128)(2,1)} %refs_6_.7) | copy-start | bytes 4423684
  14.1 4.6 %collective-permute-start.5 = (bf16[32,1152]{1,0:T(8,128)(2,1)S(1)}, bf16[32,1152]{1,0:T(8,128)(2,1)S(1)}, u32[]{:S(2)}, u32[]{:S(2)}) collective-permute-start(bf16[32,1152]{1,0:T(8,128)(2,1)S(1)} %get-tuple-element.11.refs_0_), channel_id=1, source_target_pairs={{0,3},{1,2},{2,1},{3,0},{4,7},{5,6},{6,5},{7,4},{8,11},{9,10},{10,... | collective-permute-start | bytes 221192 | tf_op jit(solution)/shard_map/ppermute | solution.py:21
  15.2 5.1 %collective-permute-start.4 = (bf16[32,1152]{1,0:T(8,128)(2,1)S(1)}, bf16[32,1152]{1,0:T(8,128)(2,1)S(1)}, u32[]{:S(2)}, u32[]{:S(2)}) collective-permute-start(bf16[32,1152]{1,0:T(8,128)(2,1)S(1)} %get-tuple-element.11.refs_0_), channel_id=1, source_target_pairs={{0,2},{1,3},{2,0},{3,1},{4,6},{5,7},{6,4},{7,5},{8,10},{9,11},{10,... | collective-permute-start | bytes 221192 | tf_op jit(solution)/shard_map/ppermute | solution.py:21
  15.7 4.7 %collective-permute-start.3 = (bf16[32,1152]{1,0:T(8,128)(2,1)S(1)}, bf16[32,1152]{1,0:T(8,128)(2,1)S(1)}, u32[]{:S(2)}, u32[]{:S(2)}) collective-permute-start(bf16[32,1152]{1,0:T(8,128)(2,1)S(1)} %get-tuple-element.11.refs_0_), channel_id=1, source_target_pairs={{0,1},{1,0},{2,3},{3,2},{4,5},{5,4},{6,7},{7,6},{8,9},{9,8},{10,11... | collective-permute-start | bytes 221192 | tf_op jit(solution)/shard_map/ppermute | solution.py:21
  21.2 5.9 %collective-permute-start.8 = (bf16[32,640]{1,0:T(8,128)(2,1)S(1)}, bf16[32,640]{1,0:T(8,128)(2,1)S(1)}, u32[]{:S(2)}, u32[]{:S(2)}) collective-permute-start(bf16[32,640]{1,0:T(8,128)(2,1)S(1)} %get-tuple-element.14.refs_0_), channel_id=1, source_target_pairs={{0,12},{4,8},{8,4},{12,0},{1,13},{5,9},{9,5},{13,1},{2,14},{6,10},... | collective-permute-start | bytes 122888 | tf_op jit(solution)/shard_map/ppermute | solution.py:21
  24.9 4.9 %collective-permute-start.7 = (bf16[32,640]{1,0:T(8,128)(2,1)S(1)}, bf16[32,640]{1,0:T(8,128)(2,1)S(1)}, u32[]{:S(2)}, u32[]{:S(2)}) collective-permute-start(bf16[32,640]{1,0:T(8,128)(2,1)S(1)} %get-tuple-element.14.refs_0_), channel_id=1, source_target_pairs={{0,8},{4,12},{8,0},{12,4},{1,9},{5,13},{9,1},{13,5},{2,10},{6,14},... | collective-permute-start | bytes 122888 | tf_op jit(solution)/shard_map/ppermute | solution.py:21
  24.9 4.9 %collective-permute-start.6 = (bf16[32,640]{1,0:T(8,128)(2,1)S(1)}, bf16[32,640]{1,0:T(8,128)(2,1)S(1)}, u32[]{:S(2)}, u32[]{:S(2)}) collective-permute-start(bf16[32,640]{1,0:T(8,128)(2,1)S(1)} %get-tuple-element.14.refs_0_), channel_id=1, source_target_pairs={{0,4},{4,0},{8,12},{12,8},{1,5},{5,1},{9,13},{13,9},{2,6},{6,2},{1... | collective-permute-start | bytes 122888 | tf_op jit(solution)/shard_map/ppermute | solution.py:21
  30.7 4.6 %collective-permute-start.11 = (bf16[32,1152]{1,0:T(8,128)(2,1)S(1)}, bf16[32,1152]{1,0:T(8,128)(2,1)S(1)}, u32[]{:S(2)}, u32[]{:S(2)}) collective-permute-start(bf16[32,1152]{1,0:T(8,128)(2,1)S(1)} %get-tuple-element.16.refs_0_), channel_id=1, source_target_pairs={{0,3},{1,2},{2,1},{3,0},{4,7},{5,6},{6,5},{7,4},{8,11},{9,10},{10,... | collective-permute-start | bytes 221192 | tf_op jit(solution)/shard_map/ppermute | solution.py:21
  30.8 5.9 %collective-permute-start.10 = (bf16[32,1152]{1,0:T(8,128)(2,1)S(1)}, bf16[32,1152]{1,0:T(8,128)(2,1)S(1)}, u32[]{:S(2)}, u32[]{:S(2)}) collective-permute-start(bf16[32,1152]{1,0:T(8,128)(2,1)S(1)} %get-tuple-element.16.refs_0_), channel_id=1, source_target_pairs={{0,2},{1,3},{2,0},{3,1},{4,6},{5,7},{6,4},{7,5},{8,10},{9,11},{10,... | collective-permute-start | bytes 221192 | tf_op jit(solution)/shard_map/ppermute | solution.py:21
  32.2 4.5 %collective-permute-start.9 = (bf16[32,1152]{1,0:T(8,128)(2,1)S(1)}, bf16[32,1152]{1,0:T(8,128)(2,1)S(1)}, u32[]{:S(2)}, u32[]{:S(2)}) collective-permute-start(bf16[32,1152]{1,0:T(8,128)(2,1)S(1)} %get-tuple-element.16.refs_0_), channel_id=1, source_target_pairs={{0,1},{1,0},{2,3},{3,2},{4,5},{5,4},{6,7},{7,6},{8,9},{9,8},{10,11... | collective-permute-start | bytes 221192 | tf_op jit(solution)/shard_map/ppermute | solution.py:21
  37.5 6.3 %collective-permute-start.14 = (bf16[32,640]{1,0:T(8,128)(2,1)S(1)}, bf16[32,640]{1,0:T(8,128)(2,1)S(1)}, u32[]{:S(2)}, u32[]{:S(2)}) collective-permute-start(bf16[32,640]{1,0:T(8,128)(2,1)S(1)} %get-tuple-element.19.refs_0_), channel_id=1, source_target_pairs={{0,12},{4,8},{8,4},{12,0},{1,13},{5,9},{9,5},{13,1},{2,14},{6,10},... | collective-permute-start | bytes 122888 | tf_op jit(solution)/shard_map/ppermute | solution.py:21
  39.0 5.7 %collective-permute-start.13 = (bf16[32,640]{1,0:T(8,128)(2,1)S(1)}, bf16[32,640]{1,0:T(8,128)(2,1)S(1)}, u32[]{:S(2)}, u32[]{:S(2)}) collective-permute-start(bf16[32,640]{1,0:T(8,128)(2,1)S(1)} %get-tuple-element.19.refs_0_), channel_id=1, source_target_pairs={{0,8},{4,12},{8,0},{12,4},{1,9},{5,13},{9,1},{13,5},{2,10},{6,14},... | collective-permute-start | bytes 122888 | tf_op jit(solution)/shard_map/ppermute | solution.py:21
  39.7 5.0 %collective-permute-start.12 = (bf16[32,640]{1,0:T(8,128)(2,1)S(1)}, bf16[32,640]{1,0:T(8,128)(2,1)S(1)}, u32[]{:S(2)}, u32[]{:S(2)}) collective-permute-start(bf16[32,640]{1,0:T(8,128)(2,1)S(1)} %get-tuple-element.19.refs_0_), channel_id=1, source_target_pairs={{0,4},{4,0},{8,12},{12,8},{1,5},{5,1},{9,13},{13,9},{2,6},{6,2},{1... | collective-permute-start | bytes 122888 | tf_op jit(solution)/shard_map/ppermute | solution.py:21

commit v2 on v1

--- a/solution.py
+++ b/solution.py
@@ -12,21 +12,40 @@
 ITERS = 2
 F32, BF16 = jnp.float32, jnp.bfloat16
 SHARE = ("period", "rep")
+SHARE_ORDER, UNIT_ORDER, PERIOD_ORDER = (0, 1, 2, 3), (0, 3, 1, 2), (0, 1, 3, 2)
 WHOLE = pl.BlockSpec(memory_space=pltpu.VMEM)
 
 
-def swap_all(block, axes):
+def swap_all(block, axes, order=None):
     size = lax.axis_size(axes)
-    return [
+    blocks = [block] + [
         lax.ppermute(block, axes, [(i, i ^ step) for i in range(size)]) for step in range(1, size)
     ]
+    return [blocks[step] for step in order] if order and size == len(order) else blocks
 
 
-def tree_sum(refs):
-    blocks = [ref[...].astype(F32) for ref in refs]
+def unordered(refs, order):
+    blocks = [ref[...] for ref in refs]
+    if len(blocks) != len(order):
+        return blocks
+    return [blocks[order.index(step)] for step in range(len(order))]
+
+
+def tree_sum(blocks):
+    blocks = [block.astype(F32) for block in blocks]
     while len(blocks) > 1:
         blocks = [a + b for a, b in zip(blocks[::2], blocks[1::2])]
     return blocks[0]
+
+
+def by_index(blocks):
+    me = lax.axis_index(SHARE)
+    bit = 1
+    while bit < len(blocks):
+        other = (me & bit) != 0
+        blocks = [jnp.where(other, blocks[i ^ bit], block) for i, block in enumerate(blocks)]
+        bit *= 2
+    return blocks
 
 
 def masked_residual(units, periods, panel, mask):
@@ -41,15 +60,43 @@
     ).astype(BF16)
 
 
+def mask_kernel(observed, mask, raw, sems):
+    pieces, size, _ = raw.shape
+    loads = [
+        pltpu.make_async_copy(observed.at[pl.ds(i * size, size), :], raw.at[i], sems.at[i])
+        for i in range(pieces)
+    ]
+    for load in loads:
+        load.start()
+    for i, load in enumerate(loads):
+        load.wait()
+        mask[pl.ds(i * size, size), :] = raw[i].astype(F32).astype(BF16)
+
+
+def mask_of(observed, pieces=4):
+    units, periods = observed.shape
+    return pl.pallas_call(
+        mask_kernel,
+        in_specs=[pl.BlockSpec(memory_space=pltpu.HBM)],
+        out_specs=WHOLE,
+        out_shape=jax.ShapeDtypeStruct(observed.shape, BF16),
+        scratch_shapes=[
+            pltpu.VMEM((pieces, units // pieces, periods), observed.dtype),
+            pltpu.SemaphoreType.DMA((pieces,)),
+        ],
+        compiler_params=pltpu.CompilerParams(vmem_limit_bytes=50 * 2**20),
+        cost_estimate=pl.CostEstimate(
+            flops=2 * units * periods, bytes_accessed=6 * units * periods, transcendentals=0
+        ),
+    )(observed)
+
+
 def first_unit_kernel(*refs):
-    *shares, period, panel, observed, mask, unit, part, rows = refs
-    me = lax.axis_index(SHARE)
+    *shares, period, panel, mask, unit, part = refs
     size = shares[0].shape[1]
-    for step, share in enumerate(shares):
-        rows[pl.ds((me ^ step) * size, size), :] = share[...].T
-    whole = rows[...].T
-    unit[...] = whole
-    mask[...] = observed[...].astype(F32).astype(BF16)
+    for place, share in enumerate(by_index(unordered(shares, SHARE_ORDER))):
+        unit[:, place * size : (place + 1) * size] = share
+    whole = unit[...]
     part[...] = unit_partial(
         whole.astype(BF16), period[...].astype(BF16), panel[...], mask[...]
     )
@@ -57,7 +104,7 @@
 
 def period_kernel(rate, *refs):
     *parts, unit, period, panel, mask, new_unit, part = refs
-    whole = unit[...] + rate * tree_sum(parts)
+    whole = unit[...] + rate * tree_sum(unordered(parts, UNIT_ORDER))
     new_unit[...] = whole
     units = whole.astype(BF16)
     residual = masked_residual(units, period[...].astype(BF16), panel[...], mask[...])
@@ -66,22 +113,22 @@
 
 def unit_kernel(rate, *refs):
     *parts, unit, period, panel, mask, new_period, part = refs
-    whole = period[...] + rate * tree_sum(parts)
+    whole = period[...] + rate * tree_sum(unordered(parts, PERIOD_ORDER))
     new_period[...] = whole
     part[...] = unit_partial(
         unit[...].astype(BF16), whole.astype(BF16), panel[...], mask[...]
     )
 
 
-def share_kernel(unit, share, rows):
+def share_kernel(unit, share):
     size = share.shape[1]
-    rows[...] = unit[...].T
-    share[...] = rows[pl.ds(lax.axis_index(SHARE) * size, size), :].T
+    count = unit.shape[1] // size
+    share[...] = by_index([unit[:, i * size : (i + 1) * size] for i in range(count)])[0]
 
 
 def last_period_kernel(rate, *refs):
     *parts, period, new_period = refs
-    new_period[...] = period[...] + rate * tree_sum(parts)
+    new_period[...] = period[...] + rate * tree_sum(unordered(parts, PERIOD_ORDER))
 
 
 def call(kernel, outs, args, scratch=()):
@@ -102,30 +149,30 @@
     unit_like, period_like = (RANK, units), (RANK, periods)
 
     own = unit_factors.T
+    mask = mask_of(observed)
     period = period_factors.T
-    mask, unit, part = call(
+    unit, part = call(
         first_unit_kernel,
-        [(panel.shape, BF16), (unit_like, F32), (unit_like, BF16)],
-        [own, *swap_all(own, SHARE), period, panel, observed],
-        [((units, RANK), F32)],
+        [(unit_like, F32), (unit_like, BF16)],
+        [*swap_all(own, SHARE, SHARE_ORDER), period, panel, mask],
     )
     for iteration in range(ITERS):
         unit, sums = call(
             functools.partial(period_kernel, unit_rate),
             [(unit_like, F32), (period_like, BF16)],
-            [part, *swap_all(part, SHARE), unit, period, panel, mask],
+            [*swap_all(part, SHARE, UNIT_ORDER), unit, period, panel, mask],
         )
         if iteration < ITERS - 1:
             period, part = call(
                 functools.partial(unit_kernel, period_rate),
                 [(period_like, F32), (unit_like, BF16)],
-                [sums, *swap_all(sums, "unit"), unit, period, panel, mask],
+                [*swap_all(sums, "unit", PERIOD_ORDER), unit, period, panel, mask],
             )
-    (share,) = call(share_kernel, [(own.shape, F32)], [unit], [((units, RANK), F32)])
+    (share,) = call(share_kernel, [(own.shape, F32)], [unit])
     (period,) = call(
         functools.partial(last_period_kernel, period_rate),
         [(period_like, F32)],
-        [sums, *swap_all(sums, "unit"), period],
+        [*swap_all(sums, "unit", PERIOD_ORDER), period],
     )
     return share.T, period.T
 

time: 45.7 us -> 38.9 us (0.85)
  local copies, waits for them, and re-layouts: 4.89 us -> 0.01 us
  waiting for transfers between devices: 18.1 us -> 15.7 us
  Pallas kernels: 5.83 us -> 6.93 us
  starting transfers between devices: 15.9 us -> 15.3 us
    unnamed x10 -> x6, local copies, waits for them, and re-layouts: 4.89 us -> 0.01 us
    ppermute x15, waiting for transfers between devices: 18.1 us -> 15.7 us  [swap_all(): lax.ppermute(block, axes, [(i, i ^ step) for i in range(size)])]
    pallas_call x0 -> x1, Pallas kernels: none -> 1.85 us  [mask_of(): pl.pallas_call(mask_kernel, in_specs=[pl.BlockSpec(memory_space=pltpu.HBM...]
    pallas_call x6, Pallas kernels: 5.83 us -> 5.07 us  [call(): pl.pallas_call(kernel, in_specs=[WHOLE] * len(args), out_specs=[WHOLE] *...]
    ppermute x15, starting transfers between devices: 15.9 us -> 15.3 us  [swap_all(): lax.ppermute(block, axes, [(i, i ^ step) for i in range(size)])]
  transfers between devices with their start and end apart: 15 -> 15, of which waited for: 10 -> 9; matrix products, arithmetic and copies ran while one was open for 0% -> 0% of each run, Pallas kernels for 2% -> 7%
where the time goes in v2:
time: 38.9 us; the launch traced here: 38.7 us
  waiting for transfers between devices  15.7 us (40%)
  starting transfers between devices  15.3 us (39%)
  Pallas kernels  6.93 us (18%)
  between operations  0.73 us (2%)
    ppermute x15, waiting for transfers between devices, swap_all(): lax.ppermute(block, axes, [(i, i ^ step) for i in range(size)])  15.7 us
    ppermute x15, starting transfers between devices, swap_all(): lax.ppermute(block, axes, [(i, i ^ step) for i in range(size)])  15.3 us
    pallas_call x6, Pallas kernels, call(): pl.pallas_call(kernel, in_specs=[WHOLE] * len(args), out_specs=[WHOLE] *...  5.07 us
    pallas_call x1, Pallas kernels, mask_of(): pl.pallas_call(mask_kernel, in_specs=[pl.BlockSpec(memory_space=pltpu.HBM...  1.85 us
  transfers between devices with their start and end apart: 15, of which 9 were waited for; matrix products, arithmetic and copies ran while one was open for 0% of the time, Pallas kernels for 7%

profile of v2, /device:TPU:0, one launch (start us, length us, event | category | flops | bytes accessed | tf_op | source)
XLA Modules:
  0.0 38.7 jit_solution(12107820753567502096)
XLA Ops:
  0.6 0.0 copy-start
  0.6 0.0 copy-start.1
  0.7 0.0 copy-start.2
  0.7 2.4 %collective-permute-start.2 = (f32[32,288]{1,0:T(8,128)}, f32[32,288]{1,0:T(8,128)S(1)}, u32[]{:S(2)}, u32[]{:S(2)}) collective-permute-start(f32[32,288]{1,0:T(8,128)} %bitcast.7), channel_id=1, source_target_pairs={{0,3},{1,2},{2,1},{3,0},{4,7},{5,6},{6,5},{7,4},{8,11},{9,10},{10,... | collective-permute-start | bytes 110600 | tf_op jit(solution)/shard_map/ppermute | solution.py:22
  3.1 0.6 %collective-permute-start.1 = (f32[32,288]{1,0:T(8,128)}, f32[32,288]{1,0:T(8,128)S(1)}, u32[]{:S(2)}, u32[]{:S(2)}) collective-permute-start(f32[32,288]{1,0:T(8,128)} %bitcast.8), channel_id=1, source_target_pairs={{0,2},{1,3},{2,0},{3,1},{4,6},{5,7},{6,4},{7,5},{8,10},{9,11},{10,... | collective-permute-start | bytes 110600 | tf_op jit(solution)/shard_map/ppermute | solution.py:22
  3.7 0.0 collective-permute-start
  3.8 1.9 %shard_map.59.refs_6_.refs_7_ = bf16[1152,640]{1,0:T(8,128)(2,1)S(1)} custom-call(s32[1152,640]{1,0:T(8,128)} %observed.1), custom_call_target="tpu_custom_call" | custom-call | flops 1474560 | bytes 4423680 | tf_op jit(solution)/shard_map/pallas_call | solution.py:78
  5.6 0.0 collective-permute-done.2.refs_3_
  5.7 2.0 %collective-permute-done.1.refs_2_ = f32[32,288]{1,0:T(8,128)S(1)} collective-permute-done((f32[32,288]{1,0:T(8,128)}, f32[32,288]{1,0:T(8,128)S(1)}, u32[]{:S(2)}, u32[]{:S(2)}) %collective-permute-start.1) | collective-permute-done | bytes 36896 | tf_op jit(solution)/shard_map/ppermute | solution.py:22
  7.6 0.0 collective-permute-done.refs_1_
  7.6 0.0 copy-done
  7.6 0.0 copy-done.1
  7.6 0.0 copy-done.2
  7.7 1.1 %shard_map.60 = (f32[32,1152]{1,0:T(8,128)S(1)}, bf16[32,1152]{1,0:T(8,128)(2,1)S(1)}) custom-call(f32[32,288]{1,0:T(8,128)S(1)} %bitcast.10, f32[32,288]{1,0:T(8,128)S(1)} %collective-permute-done.refs_1_, f32[32,288]{1,0:T(8,128)S(1)} %collective-permute-done.1.refs_2_, f32[32,288]{1,0:T(8,128)S(1)} %collective-permute-done.2.refs_3_, ...), custom_call_target="tpu_custom_call" | custom-call | tf_op jit(solution)/shard_map/pallas_call | solution.py:135
  8.8 1.4 %collective-permute-start.5 = (bf16[32,1152]{1,0:T(8,128)(2,1)S(1)}, bf16[32,1152]{1,0:T(8,128)(2,1)S(1)}, u32[]{:S(2)}, u32[]{:S(2)}) collective-permute-start(bf16[32,1152]{1,0:T(8,128)(2,1)S(1)} %get-tuple-element.10.refs_0_), channel_id=1, source_target_pairs={{0,2},{1,3},{2,0},{3,1},{4,6},{5,7},{6,4},{7,5},{8,10},{9,11},{10,... | collective-permute-start | bytes 221192 | tf_op jit(solution)/shard_map/ppermute | solution.py:22
  10.2 0.0 collective-permute-start.4
  10.2 0.8 %collective-permute-start.3 = (bf16[32,1152]{1,0:T(8,128)(2,1)S(1)}, bf16[32,1152]{1,0:T(8,128)(2,1)S(1)}, u32[]{:S(2)}, u32[]{:S(2)}) collective-permute-start(bf16[32,1152]{1,0:T(8,128)(2,1)S(1)} %get-tuple-element.10.refs_0_), channel_id=1, source_target_pairs={{0,3},{1,2},{2,1},{3,0},{4,7},{5,6},{6,5},{7,4},{8,11},{9,10},{10,... | collective-permute-start | bytes 221192 | tf_op jit(solution)/shard_map/ppermute | solution.py:22
  11.0 2.3 %collective-permute-done.5.refs_3_ = bf16[32,1152]{1,0:T(8,128)(2,1)S(1)} collective-permute-done((bf16[32,1152]{1,0:T(8,128)(2,1)S(1)}, bf16[32,1152]{1,0:T(8,128)(2,1)S(1)}, u32[]{:S(2)}, u32[]{:S(2)}) %collective-permute-start.5) | collective-permute-done | bytes 73760 | tf_op jit(solution)/shard_map/ppermute | solution.py:22
  13.3 0.0 collective-permute-done.4.refs_2_
  13.3 0.9 %collective-permute-done.3.refs_1_ = bf16[32,1152]{1,0:T(8,128)(2,1)S(1)} collective-permute-done((bf16[32,1152]{1,0:T(8,128)(2,1)S(1)}, bf16[32,1152]{1,0:T(8,128)(2,1)S(1)}, u32[]{:S(2)}, u32[]{:S(2)}) %collective-permute-start.3) | collective-permute-done | bytes 73760 | tf_op jit(solution)/shard_map/ppermute | solution.py:22
  14.2 0.8 %shard_map.61 = (f32[32,1152]{1,0:T(8,128)S(1)}, bf16[32,640]{1,0:T(8,128)(2,1)S(1)}) custom-call(bf16[32,1152]{1,0:T(8,128)(2,1)S(1)} %get-tuple-element.10.refs_0_, bf16[32,1152]{1,0:T(8,128)(2,1)S(1)} %collective-permute-done.3.refs_1_, bf16[32,1152]{1,0:T(8,128)(2,1)S(1)} %collective-permute-done.4.refs_2_, ...), custom_call_target="tpu_custom_call" | custom-call | tf_op jit(solution)/shard_map/pallas_call | solution.py:135
  14.9 2.6 %collective-permute-start.8 = (bf16[32,640]{1,0:T(8,128)(2,1)S(1)}, bf16[32,640]{1,0:T(8,128)(2,1)S(1)}, u32[]{:S(2)}, u32[]{:S(2)}) collective-permute-start(bf16[32,640]{1,0:T(8,128)(2,1)S(1)} %get-tuple-element.12.refs_0_), channel_id=1, source_target_pairs={{0,8},{4,12},{8,0},{12,4},{1,9},{5,13},{9,1},{13,5},{2,10},{6,14},... | collective-permute-start | bytes 122888 | tf_op jit(solution)/shard_map/ppermute | solution.py:22
  17.6 1.4 %collective-permute-start.7 = (bf16[32,640]{1,0:T(8,128)(2,1)S(1)}, bf16[32,640]{1,0:T(8,128)(2,1)S(1)}, u32[]{:S(2)}, u32[]{:S(2)}) collective-permute-start(bf16[32,640]{1,0:T(8,128)(2,1)S(1)} %get-tuple-element.12.refs_0_), channel_id=1, source_target_pairs={{0,12},{4,8},{8,4},{12,0},{1,13},{5,9},{9,5},{13,1},{2,14},{6,10},... | collective-permute-start | bytes 122888 | tf_op jit(solution)/shard_map/ppermute | solution.py:22
  19.0 0.2 collective-permute-start.6
  19.2 0.8 %collective-permute-done.8.refs_3_ = bf16[32,640]{1,0:T(8,128)(2,1)S(1)} collective-permute-done((bf16[32,640]{1,0:T(8,128)(2,1)S(1)}, bf16[32,640]{1,0:T(8,128)(2,1)S(1)}, u32[]{:S(2)}, u32[]{:S(2)}) %collective-permute-start.8) | collective-permute-done | bytes 40992 | tf_op jit(solution)/shard_map/ppermute | solution.py:22
  19.9 3.6 %collective-permute-done.7.refs_2_ = bf16[32,640]{1,0:T(8,128)(2,1)S(1)} collective-permute-done((bf16[32,640]{1,0:T(8,128)(2,1)S(1)}, bf16[32,640]{1,0:T(8,128)(2,1)S(1)}, u32[]{:S(2)}, u32[]{:S(2)}) %collective-permute-start.7) | collective-permute-done | bytes 40992 | tf_op jit(solution)/shard_map/ppermute | solution.py:22
  23.5 0.0 collective-permute-done.6.refs_1_
  23.5 0.9 %shard_map.62 = (f32[32,640]{1,0:T(8,128)S(1)}, bf16[32,1152]{1,0:T(8,128)(2,1)S(1)}) custom-call(bf16[32,640]{1,0:T(8,128)(2,1)S(1)} %get-tuple-element.12.refs_0_, bf16[32,640]{1,0:T(8,128)(2,1)S(1)} %collective-permute-done.6.refs_1_, bf16[32,640]{1,0:T(8,128)(2,1)S(1)} %collective-permute-done.7.refs_2_, ...), custom_call_target="tpu_custom_call" | custom-call | tf_op jit(solution)/shard_map/pallas_call | solution.py:135
  24.4 1.5 %collective-permute-start.11 = (bf16[32,1152]{1,0:T(8,128)(2,1)S(1)}, bf16[32,1152]{1,0:T(8,128)(2,1)S(1)}, u32[]{:S(2)}, u32[]{:S(2)}) collective-permute-start(bf16[32,1152]{1,0:T(8,128)(2,1)S(1)} %get-tuple-element.14.refs_0_), channel_id=1, source_target_pairs={{0,2},{1,3},{2,0},{3,1},{4,6},{5,7},{6,4},{7,5},{8,10},{9,11},{10,... | collective-permute-start | bytes 221192 | tf_op jit(solution)/shard_map/ppermute | solution.py:22
  25.9 0.0 collective-permute-start.10
  25.9 0.7 %collective-permute-start.9 = (bf16[32,1152]{1,0:T(8,128)(2,1)S(1)}, bf16[32,1152]{1,0:T(8,128)(2,1)S(1)}, u32[]{:S(2)}, u32[]{:S(2)}) collective-permute-start(bf16[32,1152]{1,0:T(8,128)(2,1)S(1)} %get-tuple-element.14.refs_0_), channel_id=1, source_target_pairs={{0,3},{1,2},{2,1},{3,0},{4,7},{5,6},{6,5},{7,4},{8,11},{9,10},{10,... | collective-permute-start | bytes 221192 | tf_op jit(solution)/shard_map/ppermute | solution.py:22
  26.6 2.2 %collective-permute-done.11.refs_3_ = bf16[32,1152]{1,0:T(8,128)(2,1)S(1)} collective-permute-done((bf16[32,1152]{1,0:T(8,128)(2,1)S(1)}, bf16[32,1152]{1,0:T(8,128)(2,1)S(1)}, u32[]{:S(2)}, u32[]{:S(2)}) %collective-permute-start.11) | collective-permute-done | bytes 73760 | tf_op jit(solution)/shard_map/ppermute | solution.py:22
  28.8 0.0 collective-permute-done.10.refs_2_
  28.8 1.0 %collective-permute-done.9.refs_1_ = bf16[32,1152]{1,0:T(8,128)(2,1)S(1)} collective-permute-done((bf16[32,1152]{1,0:T(8,128)(2,1)S(1)}, bf16[32,1152]{1,0:T(8,128)(2,1)S(1)}, u32[]{:S(2)}, u32[]{:S(2)}) %collective-permute-start.9) | collective-permute-done | bytes 73760 | tf_op jit(solution)/shard_map/ppermute | solution.py:22
  29.8 0.8 %shard_map.63 = (f32[32,1152]{1,0:T(8,128)S(1)}, bf16[32,640]{1,0:T(8,128)(2,1)S(1)}) custom-call(bf16[32,1152]{1,0:T(8,128)(2,1)S(1)} %get-tuple-element.14.refs_0_, bf16[32,1152]{1,0:T(8,128)(2,1)S(1)} %collective-permute-done.9.refs_1_, bf16[32,1152]{1,0:T(8,128)(2,1)S(1)} %collective-permute-done.10.refs_2_, ...), custom_call_target="tpu_custom_call" | custom-call | tf_op jit(solution)/shard_map/pallas_call | solution.py:135
  30.6 1.6 %collective-permute-start.14 = (bf16[32,640]{1,0:T(8,128)(2,1)S(1)}, bf16[32,640]{1,0:T(8,128)(2,1)S(1)}, u32[]{:S(2)}, u32[]{:S(2)}) collective-permute-start(bf16[32,640]{1,0:T(8,128)(2,1)S(1)} %get-tuple-element.17.refs_0_), channel_id=1, source_target_pairs={{0,8},{4,12},{8,0},{12,4},{1,9},{5,13},{9,1},{13,5},{2,10},{6,14},... | collective-permute-start | bytes 122888 | tf_op jit(solution)/shard_map/ppermute | solution.py:22
  32.2 1.0 %collective-permute-start.13 = (bf16[32,640]{1,0:T(8,128)(2,1)S(1)}, bf16[32,640]{1,0:T(8,128)(2,1)S(1)}, u32[]{:S(2)}, u32[]{:S(2)}) collective-permute-start(bf16[32,640]{1,0:T(8,128)(2,1)S(1)} %get-tuple-element.17.refs_0_), channel_id=1, source_target_pairs={{0,12},{4,8},{8,4},{12,0},{1,13},{5,9},{9,5},{13,1},{2,14},{6,10},... | collective-permute-start | bytes 122888 | tf_op jit(solution)/shard_map/ppermute | solution.py:22
  33.2 1.0 %collective-permute-start.12 = (bf16[32,640]{1,0:T(8,128)(2,1)S(1)}, bf16[32,640]{1,0:T(8,128)(2,1)S(1)}, u32[]{:S(2)}, u32[]{:S(2)}) collective-permute-start(bf16[32,640]{1,0:T(8,128)(2,1)S(1)} %get-tuple-element.17.refs_0_), channel_id=1, source_target_pairs={{0,4},{4,0},{8,12},{12,8},{1,5},{5,1},{9,13},{13,9},{2,6},{6,2},{1... | collective-permute-start | bytes 122888 | tf_op jit(solution)/shard_map/ppermute | solution.py:22
  34.1 0.8 %shard_map.64 = f32[32,288]{1,0:T(8,128)} custom-call(f32[32,1152]{1,0:T(8,128)S(1)} %get-tuple-element.16.unit), custom_call_target="tpu_custom_call" | custom-call | tf_op jit(solution)/shard_map/pallas_call | solution.py:135
  35.0 1.2 %collective-permute-done.14.refs_3_ = bf16[32,640]{1,0:T(8,128)(2,1)S(1)} collective-permute-done((bf16[32,640]{1,0:T(8,128)(2,1)S(1)}, bf16[32,640]{1,0:T(8,128)(2,1)S(1)}, u32[]{:S(2)}, u32[]{:S(2)}) %collective-permute-start.14) | collective-permute-done | bytes 40992 | tf_op jit(solution)/shard_map/ppermute | solution.py:22
  36.2 1.9 %collective-permute-done.13.refs_2_ = bf16[32,640]{1,0:T(8,128)(2,1)S(1)} collective-permute-done((bf16[32,640]{1,0:T(8,128)(2,1)S(1)}, bf16[32,640]{1,0:T(8,128)(2,1)S(1)}, u32[]{:S(2)}, u32[]{:S(2)}) %collective-permute-start.13) | collective-permute-done | bytes 40992 | tf_op jit(solution)/shard_map/ppermute | solution.py:22
  38.0 0.0 collective-permute-done.12.refs_1_
  38.0 0.7 %shard_map.65 = f32[32,640]{1,0:T(8,128)} custom-call(bf16[32,640]{1,0:T(8,128)(2,1)S(1)} %get-tuple-element.17.refs_0_, bf16[32,640]{1,0:T(8,128)(2,1)S(1)} %collective-permute-done.12.refs_1_, bf16[32,640]{1,0:T(8,128)(2,1)S(1)} %collective-permute-done.13.refs_2_, bf16[32,640]{1,0:T(8,128)(2,1)S(1)} %collective-permute-done.14.refs_3_, ...), custom_call_target="tpu_custom_call" | custom-call | tf_op jit(solution)/shard_map/pallas_call | solution.py:135
Async XLA Ops:
  0.6 7.0 %copy-start = (bf16[1152,640]{1,0:T(8,128)(2,1)S(1)}, bf16[1152,640]{1,0:T(8,128)(2,1)}, u32[]{:S(2)}) copy-start(bf16[1152,640]{1,0:T(8,128)(2,1)} %refs_6_.5) | copy-start | bytes 4423684
  0.6 7.0 %copy-start.1 = (f32[640,32]{0,1:T(8,128)S(1)}, f32[640,32]{0,1:T(8,128)}, u32[]{:S(2)}) copy-start(f32[640,32]{0,1:T(8,128)} %param.7) | copy-start | bytes 245764
  0.7 7.0 %copy-start.2 = (f32[288,32]{0,1:T(8,128)S(1)}, f32[288,32]{0,1:T(8,128)}, u32[]{:S(2)}) copy-start(f32[288,32]{0,1:T(8,128)} %param.6) | copy-start | bytes 110596
  0.7 5.0 %collective-permute-start.2 = (f32[32,288]{1,0:T(8,128)}, f32[32,288]{1,0:T(8,128)S(1)}, u32[]{:S(2)}, u32[]{:S(2)}) collective-permute-start(f32[32,288]{1,0:T(8,128)} %bitcast.7), channel_id=1, source_target_pairs={{0,3},{1,2},{2,1},{3,0},{4,7},{5,6},{6,5},{7,4},{8,11},{9,10},{10,... | collective-permute-start | bytes 110600 | tf_op jit(solution)/shard_map/ppermute | solution.py:22
  3.1 4.5 %collective-permute-start.1 = (f32[32,288]{1,0:T(8,128)}, f32[32,288]{1,0:T(8,128)S(1)}, u32[]{:S(2)}, u32[]{:S(2)}) collective-permute-start(f32[32,288]{1,0:T(8,128)} %bitcast.8), channel_id=1, source_target_pairs={{0,2},{1,3},{2,0},{3,1},{4,6},{5,7},{6,4},{7,5},{8,10},{9,11},{10,... | collective-permute-start | bytes 110600 | tf_op jit(solution)/shard_map/ppermute | solution.py:22
  3.7 3.9 %collective-permute-start = (f32[32,288]{1,0:T(8,128)}, f32[32,288]{1,0:T(8,128)S(1)}, u32[]{:S(2)}, u32[]{:S(2)}) collective-permute-start(f32[32,288]{1,0:T(8,128)} %bitcast.9), channel_id=1, source_target_pairs={{0,1},{1,0},{2,3},{3,2},{4,5},{5,4},{6,7},{7,6},{8,9},{9,8},{10,11... | collective-permute-start | bytes 110600 | tf_op jit(solution)/shard_map/ppermute | solution.py:22
  8.8 4.5 %collective-permute-start.5 = (bf16[32,1152]{1,0:T(8,128)(2,1)S(1)}, bf16[32,1152]{1,0:T(8,128)(2,1)S(1)}, u32[]{:S(2)}, u32[]{:S(2)}) collective-permute-start(bf16[32,1152]{1,0:T(8,128)(2,1)S(1)} %get-tuple-element.10.refs_0_), channel_id=1, source_target_pairs={{0,2},{1,3},{2,0},{3,1},{4,6},{5,7},{6,4},{7,5},{8,10},{9,11},{10,... | collective-permute-start | bytes 221192 | tf_op jit(solution)/shard_map/ppermute | solution.py:22
  10.2 3.1 %collective-permute-start.4 = (bf16[32,1152]{1,0:T(8,128)(2,1)S(1)}, bf16[32,1152]{1,0:T(8,128)(2,1)S(1)}, u32[]{:S(2)}, u32[]{:S(2)}) collective-permute-start(bf16[32,1152]{1,0:T(8,128)(2,1)S(1)} %get-tuple-element.10.refs_0_), channel_id=1, source_target_pairs={{0,1},{1,0},{2,3},{3,2},{4,5},{5,4},{6,7},{7,6},{8,9},{9,8},{10,11... | collective-permute-start | bytes 221192 | tf_op jit(solution)/shard_map/ppermute | solution.py:22
  10.2 4.0 %collective-permute-start.3 = (bf16[32,1152]{1,0:T(8,128)(2,1)S(1)}, bf16[32,1152]{1,0:T(8,128)(2,1)S(1)}, u32[]{:S(2)}, u32[]{:S(2)}) collective-permute-start(bf16[32,1152]{1,0:T(8,128)(2,1)S(1)} %get-tuple-element.10.refs_0_), channel_id=1, source_target_pairs={{0,3},{1,2},{2,1},{3,0},{4,7},{5,6},{6,5},{7,4},{8,11},{9,10},{10,... | collective-permute-start | bytes 221192 | tf_op jit(solution)/shard_map/ppermute | solution.py:22
  14.9 5.0 %collective-permute-start.8 = (bf16[32,640]{1,0:T(8,128)(2,1)S(1)}, bf16[32,640]{1,0:T(8,128)(2,1)S(1)}, u32[]{:S(2)}, u32[]{:S(2)}) collective-permute-start(bf16[32,640]{1,0:T(8,128)(2,1)S(1)} %get-tuple-element.12.refs_0_), channel_id=1, source_target_pairs={{0,8},{4,12},{8,0},{12,4},{1,9},{5,13},{9,1},{13,5},{2,10},{6,14},... | collective-permute-start | bytes 122888 | tf_op jit(solution)/shard_map/ppermute | solution.py:22
  17.6 5.9 %collective-permute-start.7 = (bf16[32,640]{1,0:T(8,128)(2,1)S(1)}, bf16[32,640]{1,0:T(8,128)(2,1)S(1)}, u32[]{:S(2)}, u32[]{:S(2)}) collective-permute-start(bf16[32,640]{1,0:T(8,128)(2,1)S(1)} %get-tuple-element.12.refs_0_), channel_id=1, source_target_pairs={{0,12},{4,8},{8,4},{12,0},{1,13},{5,9},{9,5},{13,1},{2,14},{6,10},... | collective-permute-start | bytes 122888 | tf_op jit(solution)/shard_map/ppermute | solution.py:22
  19.0 4.5 %collective-permute-start.6 = (bf16[32,640]{1,0:T(8,128)(2,1)S(1)}, bf16[32,640]{1,0:T(8,128)(2,1)S(1)}, u32[]{:S(2)}, u32[]{:S(2)}) collective-permute-start(bf16[32,640]{1,0:T(8,128)(2,1)S(1)} %get-tuple-element.12.refs_0_), channel_id=1, source_target_pairs={{0,4},{4,0},{8,12},{12,8},{1,5},{5,1},{9,13},{13,9},{2,6},{6,2},{1... | collective-permute-start | bytes 122888 | tf_op jit(solution)/shard_map/ppermute | solution.py:22
  24.4 4.4 %collective-permute-start.11 = (bf16[32,1152]{1,0:T(8,128)(2,1)S(1)}, bf16[32,1152]{1,0:T(8,128)(2,1)S(1)}, u32[]{:S(2)}, u32[]{:S(2)}) collective-permute-start(bf16[32,1152]{1,0:T(8,128)(2,1)S(1)} %get-tuple-element.14.refs_0_), channel_id=1, source_target_pairs={{0,2},{1,3},{2,0},{3,1},{4,6},{5,7},{6,4},{7,5},{8,10},{9,11},{10,... | collective-permute-start | bytes 221192 | tf_op jit(solution)/shard_map/ppermute | solution.py:22
  25.9 3.0 %collective-permute-start.10 = (bf16[32,1152]{1,0:T(8,128)(2,1)S(1)}, bf16[32,1152]{1,0:T(8,128)(2,1)S(1)}, u32[]{:S(2)}, u32[]{:S(2)}) collective-permute-start(bf16[32,1152]{1,0:T(8,128)(2,1)S(1)} %get-tuple-element.14.refs_0_), channel_id=1, source_target_pairs={{0,1},{1,0},{2,3},{3,2},{4,5},{5,4},{6,7},{7,6},{8,9},{9,8},{10,11... | collective-permute-start | bytes 221192 | tf_op jit(solution)/shard_map/ppermute | solution.py:22
  25.9 3.9 %collective-permute-start.9 = (bf16[32,1152]{1,0:T(8,128)(2,1)S(1)}, bf16[32,1152]{1,0:T(8,128)(2,1)S(1)}, u32[]{:S(2)}, u32[]{:S(2)}) collective-permute-start(bf16[32,1152]{1,0:T(8,128)(2,1)S(1)} %get-tuple-element.14.refs_0_), channel_id=1, source_target_pairs={{0,3},{1,2},{2,1},{3,0},{4,7},{5,6},{6,5},{7,4},{8,11},{9,10},{10,... | collective-permute-start | bytes 221192 | tf_op jit(solution)/shard_map/ppermute | solution.py:22
  30.6 5.6 %collective-permute-start.14 = (bf16[32,640]{1,0:T(8,128)(2,1)S(1)}, bf16[32,640]{1,0:T(8,128)(2,1)S(1)}, u32[]{:S(2)}, u32[]{:S(2)}) collective-permute-start(bf16[32,640]{1,0:T(8,128)(2,1)S(1)} %get-tuple-element.17.refs_0_), channel_id=1, source_target_pairs={{0,8},{4,12},{8,0},{12,4},{1,9},{5,13},{9,1},{13,5},{2,10},{6,14},... | collective-permute-start | bytes 122888 | tf_op jit(solution)/shard_map/ppermute | solution.py:22
  32.2 5.9 %collective-permute-start.13 = (bf16[32,640]{1,0:T(8,128)(2,1)S(1)}, bf16[32,640]{1,0:T(8,128)(2,1)S(1)}, u32[]{:S(2)}, u32[]{:S(2)}) collective-permute-start(bf16[32,640]{1,0:T(8,128)(2,1)S(1)} %get-tuple-element.17.refs_0_), channel_id=1, source_target_pairs={{0,12},{4,8},{8,4},{12,0},{1,13},{5,9},{9,5},{13,1},{2,14},{6,10},... | collective-permute-start | bytes 122888 | tf_op jit(solution)/shard_map/ppermute | solution.py:22
  33.2 4.9 %collective-permute-start.12 = (bf16[32,640]{1,0:T(8,128)(2,1)S(1)}, bf16[32,640]{1,0:T(8,128)(2,1)S(1)}, u32[]{:S(2)}, u32[]{:S(2)}) collective-permute-start(bf16[32,640]{1,0:T(8,128)(2,1)S(1)} %get-tuple-element.17.refs_0_), channel_id=1, source_target_pairs={{0,4},{4,0},{8,12},{12,8},{1,5},{5,1},{9,13},{13,9},{2,6},{6,2},{1... | collective-permute-start | bytes 122888 | tf_op jit(solution)/shard_map/ppermute | solution.py:22

commit v3 on v2

--- a/solution.py
+++ b/solution.py
@@ -12,7 +12,7 @@
 ITERS = 2
 F32, BF16 = jnp.float32, jnp.bfloat16
 SHARE = ("period", "rep")
-SHARE_ORDER, UNIT_ORDER, PERIOD_ORDER = (0, 1, 2, 3), (0, 3, 1, 2), (0, 1, 3, 2)
+UNIT_ORDER, PERIOD_ORDER = (0, 1, 3, 2), (0, 1, 3, 2)
 WHOLE = pl.BlockSpec(memory_space=pltpu.VMEM)
 
 
@@ -38,14 +38,20 @@
     return blocks[0]
 
 
-def by_index(blocks):
-    me = lax.axis_index(SHARE)
+def by_index(blocks, axis):
+    me = lax.axis_index(axis)
     bit = 1
     while bit < len(blocks):
         other = (me & bit) != 0
         blocks = [jnp.where(other, blocks[i ^ bit], block) for i, block in enumerate(blocks)]
         bit *= 2
     return blocks
+
+
+def lay_out(target, blocks):
+    size = blocks[0].shape[1]
+    for place, block in enumerate(blocks):
+        target[:, place * size : (place + 1) * size] = block
 
 
 def masked_residual(units, periods, panel, mask):
@@ -91,15 +97,29 @@
     )(observed)
 
 
+def chip_units(shares, step, unit, period, panel, mask):
+    lay_out(unit, by_index([share[...] for share in shares], "rep"))
+    size = unit.shape[1]
+    rows = pl.ds(pl.multiple_of((lax.axis_index("period") ^ step) * size, 16), size)
+    return unit_partial(
+        unit[...].astype(BF16), period[...].astype(BF16), panel[rows, :], mask[rows, :]
+    )
+
+
+def own_unit_kernel(share, other, period, panel, mask, unit, part):
+    part[...] = chip_units([share, other], 0, unit, period, panel, mask)
+
+
 def first_unit_kernel(*refs):
-    *shares, period, panel, mask, unit, part = refs
-    size = shares[0].shape[1]
-    for place, share in enumerate(by_index(unordered(shares, SHARE_ORDER))):
-        unit[:, place * size : (place + 1) * size] = share
-    whole = unit[...]
-    part[...] = unit_partial(
-        whole.astype(BF16), period[...].astype(BF16), panel[...], mask[...]
-    )
+    *shares, own_unit, own_part, period, panel, mask, unit, part, chips = refs
+    shares = shares[::-1]
+    units, parts = [own_unit[...]], [own_part[...]]
+    for step in range(1, chips.shape[0] + 1):
+        pair = shares[2 * step - 2 : 2 * step]
+        parts.append(chip_units(pair, step, chips.at[step - 1], period, panel, mask))
+        units.append(chips[step - 1])
+    lay_out(unit, by_index(units, "period"))
+    lay_out(part, by_index(parts, "period"))
 
 
 def period_kernel(rate, *refs):
@@ -123,7 +143,8 @@
 def share_kernel(unit, share):
     size = share.shape[1]
     count = unit.shape[1] // size
-    share[...] = by_index([unit[:, i * size : (i + 1) * size] for i in range(count)])[0]
+    blocks = [unit[:, i * size : (i + 1) * size] for i in range(count)]
+    share[...] = by_index(blocks, SHARE)[0]
 
 
 def last_period_kernel(rate, *refs):
@@ -151,10 +172,18 @@
     own = unit_factors.T
     mask = mask_of(observed)
     period = period_factors.T
+    shares = swap_all(own, SHARE)
+    chip_like = (RANK, 2 * own.shape[1])
+    unit, part = call(
+        own_unit_kernel,
+        [(chip_like, F32), (chip_like, BF16)],
+        [*shares[:2], period, panel, mask],
+    )
     unit, part = call(
         first_unit_kernel,
         [(unit_like, F32), (unit_like, BF16)],
-        [*swap_all(own, SHARE, SHARE_ORDER), period, panel, mask],
+        [*shares[:1:-1], unit, part, period, panel, mask],
+        [((units // chip_like[1] - 1, *chip_like), F32)],
     )
     for iteration in range(ITERS):
         unit, sums = call(

time: 38.9 us -> 38.6 us (level)
  waiting for transfers between devices: 15.7 us -> 15.3 us
    ppermute x15, waiting for transfers between devices: 15.7 us -> 15.3 us  [swap_all(): lax.ppermute(block, axes, [(i, i ^ step) for i in range(size)])]
    pallas_call x6 -> x7, Pallas kernels: 5.07 us -> 5.21 us  [call(): pl.pallas_call(kernel, in_specs=[WHOLE] * len(args), out_specs=[WHOLE] *...]
  transfers between devices with their start and end apart: 15 -> 15, of which waited for: 9 -> 9; matrix products, arithmetic and copies ran while one was open for 0% -> 0% of each run, Pallas kernels for 7% -> 9%
where the time goes in v3:
time: 38.6 us; the launch traced here: 38.5 us
  starting transfers between devices  15.4 us (40%)
  waiting for transfers between devices  15.3 us (40%)
  Pallas kernels  7.06 us (18%)
  between operations  0.75 us (2%)
    ppermute x15, starting transfers between devices, swap_all(): lax.ppermute(block, axes, [(i, i ^ step) for i in range(size)])  15.4 us
    ppermute x15, waiting for transfers between devices, swap_all(): lax.ppermute(block, axes, [(i, i ^ step) for i in range(size)])  15.3 us
    pallas_call x7, Pallas kernels, call(): pl.pallas_call(kernel, in_specs=[WHOLE] * len(args), out_specs=[WHOLE] *...  5.21 us
    pallas_call x1, Pallas kernels, mask_of(): pl.pallas_call(mask_kernel, in_specs=[pl.BlockSpec(memory_space=pltpu.HBM...  1.85 us
  transfers between devices with their start and end apart: 15, of which 9 were waited for; matrix products, arithmetic and copies ran while one was open for 0% of the time, Pallas kernels for 9%

profile of v3, /device:TPU:0, one launch (start us, length us, event | category | flops | bytes accessed | tf_op | source)
XLA Modules:
  0.0 38.5 jit_solution(11956721199695722960)
XLA Ops:
  0.6 0.0 copy-start
  0.6 0.0 copy-start.1
  0.7 0.0 copy-start.2
  0.7 0.5 %collective-permute-start.2 = (f32[32,288]{1,0:T(8,128)}, f32[32,288]{1,0:T(8,128)S(1)}, u32[]{:S(2)}, u32[]{:S(2)}) collective-permute-start(f32[32,288]{1,0:T(8,128)} %bitcast.8), channel_id=1, source_target_pairs={{0,1},{1,0},{2,3},{3,2},{4,5},{5,4},{6,7},{7,6},{8,9},{9,8},{10,11... | collective-permute-start | bytes 110600 | tf_op jit(solution)/shard_map/ppermute | solution.py:22
  1.2 2.6 %collective-permute-start.1 = (f32[32,288]{1,0:T(8,128)}, f32[32,288]{1,0:T(8,128)S(1)}, u32[]{:S(2)}, u32[]{:S(2)}) collective-permute-start(f32[32,288]{1,0:T(8,128)} %bitcast.9), channel_id=1, source_target_pairs={{0,2},{1,3},{2,0},{3,1},{4,6},{5,7},{6,4},{7,5},{8,10},{9,11},{10,... | collective-permute-start | bytes 110600 | tf_op jit(solution)/shard_map/ppermute | solution.py:22
  3.7 0.1 collective-permute-start
  3.8 1.9 %shard_map.59.mask.refs_6_.refs_7_ = bf16[1152,640]{1,0:T(8,128)(2,1)S(1)} custom-call(s32[1152,640]{1,0:T(8,128)} %observed.1), custom_call_target="tpu_custom_call" | custom-call | flops 1474560 | bytes 4423680 | tf_op jit(solution)/shard_map/pallas_call | solution.py:84
  5.7 0.0 collective-permute-done.2.other
  5.7 0.0 copy-done
  5.7 0.0 copy-done.1
  5.7 0.0 copy-done.2
  5.7 0.6 %shard_map.60 = (f32[32,576]{1,0:T(8,128)S(1)}, bf16[32,576]{1,0:T(8,128)(2,1)S(1)}) custom-call(f32[32,288]{1,0:T(8,128)S(1)} %bitcast.11, f32[32,288]{1,0:T(8,128)S(1)} %collective-permute-done.2.other, f32[32,640]{1,0:T(8,128)S(1)} %bitcast.4, bf16[1152,640]{1,0:T(8,128)(2,1)S(1)} %copy-done, bf16[1152,640]{1,0:T(8,128)(2,1)S(1)} %shard_map.59.mask.refs_6_.refs_7_), custom_call_target="tpu_custom_call" | custom-call | tf_op jit(solution)/shard_map/pallas_call | solution.py:156
  6.3 0.0 collective-permute-done.1.refs_1_
  6.3 1.4 %collective-permute-done.refs_0_ = f32[32,288]{1,0:T(8,128)S(1)} collective-permute-done((f32[32,288]{1,0:T(8,128)}, f32[32,288]{1,0:T(8,128)S(1)}, u32[]{:S(2)}, u32[]{:S(2)}) %collective-permute-start) | collective-permute-done | bytes 36896 | tf_op jit(solution)/shard_map/ppermute | solution.py:22
  7.7 0.7 %shard_map.61 = (f32[32,1152]{1,0:T(8,128)S(1)}, bf16[32,1152]{1,0:T(8,128)(2,1)S(1)}) custom-call(f32[32,288]{1,0:T(8,128)S(1)} %collective-permute-done.refs_0_, f32[32,288]{1,0:T(8,128)S(1)} %collective-permute-done.1.refs_1_, f32[32,576]{1,0:T(8,128)S(1)} %get-tuple-element.12.refs_2_, bf16[32,576]{1,0:T(8,128)(2,1)S(1)} %get-tuple-element.13.refs_3_, ...), custom_call_target="tpu_custom_call" | custom-call | tf_op jit(solution)/shard_map/pallas_call | solution.py:156
  8.4 1.0 %collective-permute-start.5 = (bf16[32,1152]{1,0:T(8,128)(2,1)S(1)}, bf16[32,1152]{1,0:T(8,128)(2,1)S(1)}, u32[]{:S(2)}, u32[]{:S(2)}) collective-permute-start(bf16[32,1152]{1,0:T(8,128)(2,1)S(1)} %get-tuple-element.14.refs_0_), channel_id=1, source_target_pairs={{0,2},{1,3},{2,0},{3,1},{4,6},{5,7},{6,4},{7,5},{8,10},{9,11},{10,... | collective-permute-start | bytes 221192 | tf_op jit(solution)/shard_map/ppermute | solution.py:22
  9.4 0.6 %collective-permute-start.4 = (bf16[32,1152]{1,0:T(8,128)(2,1)S(1)}, bf16[32,1152]{1,0:T(8,128)(2,1)S(1)}, u32[]{:S(2)}, u32[]{:S(2)}) collective-permute-start(bf16[32,1152]{1,0:T(8,128)(2,1)S(1)} %get-tuple-element.14.refs_0_), channel_id=1, source_target_pairs={{0,3},{1,2},{2,1},{3,0},{4,7},{5,6},{6,5},{7,4},{8,11},{9,10},{10,... | collective-permute-start | bytes 221192 | tf_op jit(solution)/shard_map/ppermute | solution.py:22
  9.9 0.7 %collective-permute-start.3 = (bf16[32,1152]{1,0:T(8,128)(2,1)S(1)}, bf16[32,1152]{1,0:T(8,128)(2,1)S(1)}, u32[]{:S(2)}, u32[]{:S(2)}) collective-permute-start(bf16[32,1152]{1,0:T(8,128)(2,1)S(1)} %get-tuple-element.14.refs_0_), channel_id=1, source_target_pairs={{0,1},{1,0},{2,3},{3,2},{4,5},{5,4},{6,7},{7,6},{8,9},{9,8},{10,11... | collective-permute-start | bytes 221192 | tf_op jit(solution)/shard_map/ppermute | solution.py:22
  10.6 2.7 %collective-permute-done.5.refs_3_ = bf16[32,1152]{1,0:T(8,128)(2,1)S(1)} collective-permute-done((bf16[32,1152]{1,0:T(8,128)(2,1)S(1)}, bf16[32,1152]{1,0:T(8,128)(2,1)S(1)}, u32[]{:S(2)}, u32[]{:S(2)}) %collective-permute-start.5) | collective-permute-done | bytes 73760 | tf_op jit(solution)/shard_map/ppermute | solution.py:22
  13.3 0.7 %collective-permute-done.4.refs_2_ = bf16[32,1152]{1,0:T(8,128)(2,1)S(1)} collective-permute-done((bf16[32,1152]{1,0:T(8,128)(2,1)S(1)}, bf16[32,1152]{1,0:T(8,128)(2,1)S(1)}, u32[]{:S(2)}, u32[]{:S(2)}) %collective-permute-start.4) | collective-permute-done | bytes 73760 | tf_op jit(solution)/shard_map/ppermute | solution.py:22
  13.9 0.0 collective-permute-done.3.refs_1_
  13.9 0.8 %shard_map.62 = (f32[32,1152]{1,0:T(8,128)S(1)}, bf16[32,640]{1,0:T(8,128)(2,1)S(1)}) custom-call(bf16[32,1152]{1,0:T(8,128)(2,1)S(1)} %get-tuple-element.14.refs_0_, bf16[32,1152]{1,0:T(8,128)(2,1)S(1)} %collective-permute-done.3.refs_1_, bf16[32,1152]{1,0:T(8,128)(2,1)S(1)} %collective-permute-done.4.refs_2_, ...), custom_call_target="tpu_custom_call" | custom-call | tf_op jit(solution)/shard_map/pallas_call | solution.py:156
  14.7 2.7 %collective-permute-start.8 = (bf16[32,640]{1,0:T(8,128)(2,1)S(1)}, bf16[32,640]{1,0:T(8,128)(2,1)S(1)}, u32[]{:S(2)}, u32[]{:S(2)}) collective-permute-start(bf16[32,640]{1,0:T(8,128)(2,1)S(1)} %get-tuple-element.16.refs_0_), channel_id=1, source_target_pairs={{0,8},{4,12},{8,0},{12,4},{1,9},{5,13},{9,1},{13,5},{2,10},{6,14},... | collective-permute-start | bytes 122888 | tf_op jit(solution)/shard_map/ppermute | solution.py:22
  17.4 1.3 %collective-permute-start.7 = (bf16[32,640]{1,0:T(8,128)(2,1)S(1)}, bf16[32,640]{1,0:T(8,128)(2,1)S(1)}, u32[]{:S(2)}, u32[]{:S(2)}) collective-permute-start(bf16[32,640]{1,0:T(8,128)(2,1)S(1)} %get-tuple-element.16.refs_0_), channel_id=1, source_target_pairs={{0,12},{4,8},{8,4},{12,0},{1,13},{5,9},{9,5},{13,1},{2,14},{6,10},... | collective-permute-start | bytes 122888 | tf_op jit(solution)/shard_map/ppermute | solution.py:22
  18.7 0.2 collective-permute-start.6
  19.0 1.2 %collective-permute-done.8.refs_3_ = bf16[32,640]{1,0:T(8,128)(2,1)S(1)} collective-permute-done((bf16[32,640]{1,0:T(8,128)(2,1)S(1)}, bf16[32,640]{1,0:T(8,128)(2,1)S(1)}, u32[]{:S(2)}, u32[]{:S(2)}) %collective-permute-start.8) | collective-permute-done | bytes 40992 | tf_op jit(solution)/shard_map/ppermute | solution.py:22
  20.1 3.1 %collective-permute-done.7.refs_2_ = bf16[32,640]{1,0:T(8,128)(2,1)S(1)} collective-permute-done((bf16[32,640]{1,0:T(8,128)(2,1)S(1)}, bf16[32,640]{1,0:T(8,128)(2,1)S(1)}, u32[]{:S(2)}, u32[]{:S(2)}) %collective-permute-start.7) | collective-permute-done | bytes 40992 | tf_op jit(solution)/shard_map/ppermute | solution.py:22
  23.2 0.0 collective-permute-done.6.refs_1_
  23.2 0.9 %shard_map.63 = (f32[32,640]{1,0:T(8,128)S(1)}, bf16[32,1152]{1,0:T(8,128)(2,1)S(1)}) custom-call(bf16[32,640]{1,0:T(8,128)(2,1)S(1)} %get-tuple-element.16.refs_0_, bf16[32,640]{1,0:T(8,128)(2,1)S(1)} %collective-permute-done.6.refs_1_, bf16[32,640]{1,0:T(8,128)(2,1)S(1)} %collective-permute-done.7.refs_2_, ...), custom_call_target="tpu_custom_call" | custom-call | tf_op jit(solution)/shard_map/pallas_call | solution.py:156
  24.1 1.1 %collective-permute-start.11 = (bf16[32,1152]{1,0:T(8,128)(2,1)S(1)}, bf16[32,1152]{1,0:T(8,128)(2,1)S(1)}, u32[]{:S(2)}, u32[]{:S(2)}) collective-permute-start(bf16[32,1152]{1,0:T(8,128)(2,1)S(1)} %get-tuple-element.18.refs_0_), channel_id=1, source_target_pairs={{0,2},{1,3},{2,0},{3,1},{4,6},{5,7},{6,4},{7,5},{8,10},{9,11},{10,... | collective-permute-start | bytes 221192 | tf_op jit(solution)/shard_map/ppermute | solution.py:22
  25.2 0.0 collective-permute-start.10
  25.2 1.1 %collective-permute-start.9 = (bf16[32,1152]{1,0:T(8,128)(2,1)S(1)}, bf16[32,1152]{1,0:T(8,128)(2,1)S(1)}, u32[]{:S(2)}, u32[]{:S(2)}) collective-permute-start(bf16[32,1152]{1,0:T(8,128)(2,1)S(1)} %get-tuple-element.18.refs_0_), channel_id=1, source_target_pairs={{0,1},{1,0},{2,3},{3,2},{4,5},{5,4},{6,7},{7,6},{8,9},{9,8},{10,11... | collective-permute-start | bytes 221192 | tf_op jit(solution)/shard_map/ppermute | solution.py:22
  26.3 2.6 %collective-permute-done.11.refs_3_ = bf16[32,1152]{1,0:T(8,128)(2,1)S(1)} collective-permute-done((bf16[32,1152]{1,0:T(8,128)(2,1)S(1)}, bf16[32,1152]{1,0:T(8,128)(2,1)S(1)}, u32[]{:S(2)}, u32[]{:S(2)}) %collective-permute-start.11) | collective-permute-done | bytes 73760 | tf_op jit(solution)/shard_map/ppermute | solution.py:22
  28.9 0.8 %collective-permute-done.10.refs_2_ = bf16[32,1152]{1,0:T(8,128)(2,1)S(1)} collective-permute-done((bf16[32,1152]{1,0:T(8,128)(2,1)S(1)}, bf16[32,1152]{1,0:T(8,128)(2,1)S(1)}, u32[]{:S(2)}, u32[]{:S(2)}) %collective-permute-start.10) | collective-permute-done | bytes 73760 | tf_op jit(solution)/shard_map/ppermute | solution.py:22
  29.7 0.0 collective-permute-done.9.refs_1_
  29.7 0.8 %shard_map.64 = (f32[32,1152]{1,0:T(8,128)S(1)}, bf16[32,640]{1,0:T(8,128)(2,1)S(1)}) custom-call(bf16[32,1152]{1,0:T(8,128)(2,1)S(1)} %get-tuple-element.18.refs_0_, bf16[32,1152]{1,0:T(8,128)(2,1)S(1)} %collective-permute-done.9.refs_1_, bf16[32,1152]{1,0:T(8,128)(2,1)S(1)} %collective-permute-done.10.refs_2_, ...), custom_call_target="tpu_custom_call" | custom-call | tf_op jit(solution)/shard_map/pallas_call | solution.py:156
  30.5 1.5 %collective-permute-start.14 = (bf16[32,640]{1,0:T(8,128)(2,1)S(1)}, bf16[32,640]{1,0:T(8,128)(2,1)S(1)}, u32[]{:S(2)}, u32[]{:S(2)}) collective-permute-start(bf16[32,640]{1,0:T(8,128)(2,1)S(1)} %get-tuple-element.21.refs_0_), channel_id=1, source_target_pairs={{0,8},{4,12},{8,0},{12,4},{1,9},{5,13},{9,1},{13,5},{2,10},{6,14},... | collective-permute-start | bytes 122888 | tf_op jit(solution)/shard_map/ppermute | solution.py:22
  32.0 1.0 %collective-permute-start.13 = (bf16[32,640]{1,0:T(8,128)(2,1)S(1)}, bf16[32,640]{1,0:T(8,128)(2,1)S(1)}, u32[]{:S(2)}, u32[]{:S(2)}) collective-permute-start(bf16[32,640]{1,0:T(8,128)(2,1)S(1)} %get-tuple-element.21.refs_0_), channel_id=1, source_target_pairs={{0,12},{4,8},{8,4},{12,0},{1,13},{5,9},{9,5},{13,1},{2,14},{6,10},... | collective-permute-start | bytes 122888 | tf_op jit(solution)/shard_map/ppermute | solution.py:22
  33.0 1.1 %collective-permute-start.12 = (bf16[32,640]{1,0:T(8,128)(2,1)S(1)}, bf16[32,640]{1,0:T(8,128)(2,1)S(1)}, u32[]{:S(2)}, u32[]{:S(2)}) collective-permute-start(bf16[32,640]{1,0:T(8,128)(2,1)S(1)} %get-tuple-element.21.refs_0_), channel_id=1, source_target_pairs={{0,4},{4,0},{8,12},{12,8},{1,5},{5,1},{9,13},{13,9},{2,6},{6,2},{1... | collective-permute-start | bytes 122888 | tf_op jit(solution)/shard_map/ppermute | solution.py:22
  34.0 0.8 %shard_map.65 = f32[32,288]{1,0:T(8,128)} custom-call(f32[32,1152]{1,0:T(8,128)S(1)} %get-tuple-element.20.unit), custom_call_target="tpu_custom_call" | custom-call | tf_op jit(solution)/shard_map/pallas_call | solution.py:156
  34.9 1.0 %collective-permute-done.14.refs_3_ = bf16[32,640]{1,0:T(8,128)(2,1)S(1)} collective-permute-done((bf16[32,640]{1,0:T(8,128)(2,1)S(1)}, bf16[32,640]{1,0:T(8,128)(2,1)S(1)}, u32[]{:S(2)}, u32[]{:S(2)}) %collective-permute-start.14) | collective-permute-done | bytes 40992 | tf_op jit(solution)/shard_map/ppermute | solution.py:22
  35.9 1.9 %collective-permute-done.13.refs_2_ = bf16[32,640]{1,0:T(8,128)(2,1)S(1)} collective-permute-done((bf16[32,640]{1,0:T(8,128)(2,1)S(1)}, bf16[32,640]{1,0:T(8,128)(2,1)S(1)}, u32[]{:S(2)}, u32[]{:S(2)}) %collective-permute-start.13) | collective-permute-done | bytes 40992 | tf_op jit(solution)/shard_map/ppermute | solution.py:22
  37.8 0.0 collective-permute-done.12.refs_1_
  37.8 0.7 %shard_map.66 = f32[32,640]{1,0:T(8,128)} custom-call(bf16[32,640]{1,0:T(8,128)(2,1)S(1)} %get-tuple-element.21.refs_0_, bf16[32,640]{1,0:T(8,128)(2,1)S(1)} %collective-permute-done.12.refs_1_, bf16[32,640]{1,0:T(8,128)(2,1)S(1)} %collective-permute-done.13.refs_2_, bf16[32,640]{1,0:T(8,128)(2,1)S(1)} %collective-permute-done.14.refs_3_, ...), custom_call_target="tpu_custom_call" | custom-call | tf_op jit(solution)/shard_map/pallas_call | solution.py:156
Async XLA Ops:
  0.6 5.1 %copy-start = (bf16[1152,640]{1,0:T(8,128)(2,1)S(1)}, bf16[1152,640]{1,0:T(8,128)(2,1)}, u32[]{:S(2)}) copy-start(bf16[1152,640]{1,0:T(8,128)(2,1)} %refs_6_.5) | copy-start | bytes 4423684
  0.6 5.1 %copy-start.1 = (f32[640,32]{0,1:T(8,128)S(1)}, f32[640,32]{0,1:T(8,128)}, u32[]{:S(2)}) copy-start(f32[640,32]{0,1:T(8,128)} %param.7) | copy-start | bytes 245764
  0.7 5.1 %copy-start.2 = (f32[288,32]{0,1:T(8,128)S(1)}, f32[288,32]{0,1:T(8,128)}, u32[]{:S(2)}) copy-start(f32[288,32]{0,1:T(8,128)} %param.6) | copy-start | bytes 110596
  0.7 5.0 %collective-permute-start.2 = (f32[32,288]{1,0:T(8,128)}, f32[32,288]{1,0:T(8,128)S(1)}, u32[]{:S(2)}, u32[]{:S(2)}) collective-permute-start(f32[32,288]{1,0:T(8,128)} %bitcast.8), channel_id=1, source_target_pairs={{0,1},{1,0},{2,3},{3,2},{4,5},{5,4},{6,7},{7,6},{8,9},{9,8},{10,11... | collective-permute-start | bytes 110600 | tf_op jit(solution)/shard_map/ppermute | solution.py:22
  1.2 5.1 %collective-permute-start.1 = (f32[32,288]{1,0:T(8,128)}, f32[32,288]{1,0:T(8,128)S(1)}, u32[]{:S(2)}, u32[]{:S(2)}) collective-permute-start(f32[32,288]{1,0:T(8,128)} %bitcast.9), channel_id=1, source_target_pairs={{0,2},{1,3},{2,0},{3,1},{4,6},{5,7},{6,4},{7,5},{8,10},{9,11},{10,... | collective-permute-start | bytes 110600 | tf_op jit(solution)/shard_map/ppermute | solution.py:22
  3.7 4.0 %collective-permute-start = (f32[32,288]{1,0:T(8,128)}, f32[32,288]{1,0:T(8,128)S(1)}, u32[]{:S(2)}, u32[]{:S(2)}) collective-permute-start(f32[32,288]{1,0:T(8,128)} %bitcast.10), channel_id=1, source_target_pairs={{0,3},{1,2},{2,1},{3,0},{4,7},{5,6},{6,5},{7,4},{8,11},{9,10},{10,... | collective-permute-start | bytes 110600 | tf_op jit(solution)/shard_map/ppermute | solution.py:22
  8.4 4.9 %collective-permute-start.5 = (bf16[32,1152]{1,0:T(8,128)(2,1)S(1)}, bf16[32,1152]{1,0:T(8,128)(2,1)S(1)}, u32[]{:S(2)}, u32[]{:S(2)}) collective-permute-start(bf16[32,1152]{1,0:T(8,128)(2,1)S(1)} %get-tuple-element.14.refs_0_), channel_id=1, source_target_pairs={{0,2},{1,3},{2,0},{3,1},{4,6},{5,7},{6,4},{7,5},{8,10},{9,11},{10,... | collective-permute-start | bytes 221192 | tf_op jit(solution)/shard_map/ppermute | solution.py:22
  9.4 4.6 %collective-permute-start.4 = (bf16[32,1152]{1,0:T(8,128)(2,1)S(1)}, bf16[32,1152]{1,0:T(8,128)(2,1)S(1)}, u32[]{:S(2)}, u32[]{:S(2)}) collective-permute-start(bf16[32,1152]{1,0:T(8,128)(2,1)S(1)} %get-tuple-element.14.refs_0_), channel_id=1, source_target_pairs={{0,3},{1,2},{2,1},{3,0},{4,7},{5,6},{6,5},{7,4},{8,11},{9,10},{10,... | collective-permute-start | bytes 221192 | tf_op jit(solution)/shard_map/ppermute | solution.py:22
  9.9 4.0 %collective-permute-start.3 = (bf16[32,1152]{1,0:T(8,128)(2,1)S(1)}, bf16[32,1152]{1,0:T(8,128)(2,1)S(1)}, u32[]{:S(2)}, u32[]{:S(2)}) collective-permute-start(bf16[32,1152]{1,0:T(8,128)(2,1)S(1)} %get-tuple-element.14.refs_0_), channel_id=1, source_target_pairs={{0,1},{1,0},{2,3},{3,2},{4,5},{5,4},{6,7},{7,6},{8,9},{9,8},{10,11... | collective-permute-start | bytes 221192 | tf_op jit(solution)/shard_map/ppermute | solution.py:22
  14.7 5.4 %collective-permute-start.8 = (bf16[32,640]{1,0:T(8,128)(2,1)S(1)}, bf16[32,640]{1,0:T(8,128)(2,1)S(1)}, u32[]{:S(2)}, u32[]{:S(2)}) collective-permute-start(bf16[32,640]{1,0:T(8,128)(2,1)S(1)} %get-tuple-element.16.refs_0_), channel_id=1, source_target_pairs={{0,8},{4,12},{8,0},{12,4},{1,9},{5,13},{9,1},{13,5},{2,10},{6,14},... | collective-permute-start | bytes 122888 | tf_op jit(solution)/shard_map/ppermute | solution.py:22
  17.4 5.8 %collective-permute-start.7 = (bf16[32,640]{1,0:T(8,128)(2,1)S(1)}, bf16[32,640]{1,0:T(8,128)(2,1)S(1)}, u32[]{:S(2)}, u32[]{:S(2)}) collective-permute-start(bf16[32,640]{1,0:T(8,128)(2,1)S(1)} %get-tuple-element.16.refs_0_), channel_id=1, source_target_pairs={{0,12},{4,8},{8,4},{12,0},{1,13},{5,9},{9,5},{13,1},{2,14},{6,10},... | collective-permute-start | bytes 122888 | tf_op jit(solution)/shard_map/ppermute | solution.py:22
  18.7 4.5 %collective-permute-start.6 = (bf16[32,640]{1,0:T(8,128)(2,1)S(1)}, bf16[32,640]{1,0:T(8,128)(2,1)S(1)}, u32[]{:S(2)}, u32[]{:S(2)}) collective-permute-start(bf16[32,640]{1,0:T(8,128)(2,1)S(1)} %get-tuple-element.16.refs_0_), channel_id=1, source_target_pairs={{0,4},{4,0},{8,12},{12,8},{1,5},{5,1},{9,13},{13,9},{2,6},{6,2},{1... | collective-permute-start | bytes 122888 | tf_op jit(solution)/shard_map/ppermute | solution.py:22
  24.1 4.8 %collective-permute-start.11 = (bf16[32,1152]{1,0:T(8,128)(2,1)S(1)}, bf16[32,1152]{1,0:T(8,128)(2,1)S(1)}, u32[]{:S(2)}, u32[]{:S(2)}) collective-permute-start(bf16[32,1152]{1,0:T(8,128)(2,1)S(1)} %get-tuple-element.18.refs_0_), channel_id=1, source_target_pairs={{0,2},{1,3},{2,0},{3,1},{4,6},{5,7},{6,4},{7,5},{8,10},{9,11},{10,... | collective-permute-start | bytes 221192 | tf_op jit(solution)/shard_map/ppermute | solution.py:22
  25.2 4.5 %collective-permute-start.10 = (bf16[32,1152]{1,0:T(8,128)(2,1)S(1)}, bf16[32,1152]{1,0:T(8,128)(2,1)S(1)}, u32[]{:S(2)}, u32[]{:S(2)}) collective-permute-start(bf16[32,1152]{1,0:T(8,128)(2,1)S(1)} %get-tuple-element.18.refs_0_), channel_id=1, source_target_pairs={{0,3},{1,2},{2,1},{3,0},{4,7},{5,6},{6,5},{7,4},{8,11},{9,10},{10,... | collective-permute-start | bytes 221192 | tf_op jit(solution)/shard_map/ppermute | solution.py:22
  25.2 4.5 %collective-permute-start.9 = (bf16[32,1152]{1,0:T(8,128)(2,1)S(1)}, bf16[32,1152]{1,0:T(8,128)(2,1)S(1)}, u32[]{:S(2)}, u32[]{:S(2)}) collective-permute-start(bf16[32,1152]{1,0:T(8,128)(2,1)S(1)} %get-tuple-element.18.refs_0_), channel_id=1, source_target_pairs={{0,1},{1,0},{2,3},{3,2},{4,5},{5,4},{6,7},{7,6},{8,9},{9,8},{10,11... | collective-permute-start | bytes 221192 | tf_op jit(solution)/shard_map/ppermute | solution.py:22
  30.5 5.4 %collective-permute-start.14 = (bf16[32,640]{1,0:T(8,128)(2,1)S(1)}, bf16[32,640]{1,0:T(8,128)(2,1)S(1)}, u32[]{:S(2)}, u32[]{:S(2)}) collective-permute-start(bf16[32,640]{1,0:T(8,128)(2,1)S(1)} %get-tuple-element.21.refs_0_), channel_id=1, source_target_pairs={{0,8},{4,12},{8,0},{12,4},{1,9},{5,13},{9,1},{13,5},{2,10},{6,14},... | collective-permute-start | bytes 122888 | tf_op jit(solution)/shard_map/ppermute | solution.py:22
  32.0 5.8 %collective-permute-start.13 = (bf16[32,640]{1,0:T(8,128)(2,1)S(1)}, bf16[32,640]{1,0:T(8,128)(2,1)S(1)}, u32[]{:S(2)}, u32[]{:S(2)}) collective-permute-start(bf16[32,640]{1,0:T(8,128)(2,1)S(1)} %get-tuple-element.21.refs_0_), channel_id=1, source_target_pairs={{0,12},{4,8},{8,4},{12,0},{1,13},{5,9},{9,5},{13,1},{2,14},{6,10},... | collective-permute-start | bytes 122888 | tf_op jit(solution)/shard_map/ppermute | solution.py:22
  33.0 4.8 %collective-permute-start.12 = (bf16[32,640]{1,0:T(8,128)(2,1)S(1)}, bf16[32,640]{1,0:T(8,128)(2,1)S(1)}, u32[]{:S(2)}, u32[]{:S(2)}) collective-permute-start(bf16[32,640]{1,0:T(8,128)(2,1)S(1)} %get-tuple-element.21.refs_0_), channel_id=1, source_target_pairs={{0,4},{4,0},{8,12},{12,8},{1,5},{5,1},{9,13},{13,9},{2,6},{6,2},{1... | collective-permute-start | bytes 122888 | tf_op jit(solution)/shard_map/ppermute | solution.py:22
